TPU v7x, 32 devices: a whole 2x2x4 slice. The times are simulated.
32 devices in a mesh: grp: 2 (over y), pix: 4 (over z), chan: 2 (over x), sub: 2 (over core).
Axes of the slice: x: 2, y: 2, z: 4, core: 2. Of those that a mesh axis runs over, the one named last changes fastest.
Arguments:
- features: bfloat16 [256, 131072], P('chan', ('grp', 'pix', 'sub')), parts along dimension 1, may hold values from -6 to 6
- neighbours: int32 [8, 131072], P(None, ('grp', 'pix', 'sub')), parts along dimension 1, may hold values from 0 to 8703, as said below
- live_cols: int32 [16], P(('grp', 'pix', 'sub')), parts along dimension 0, may hold values from 8 to 32, as said below
- cheb_weight: bfloat16 [7, 256, 256], replicated, may hold values from -0.125 to 0.125
- out_bias: float32 [256], replicated, may hold values from -3 to 3
Outputs:
- mixed: bfloat16 [16, 8192, 256], P(('grp', 'pix', 'sub'), 'chan'), parts along dimension 0
There are 2 independent parts, one for each index of `grp`. A program takes and returns all parts, laid end to end along the dimension named above; an argument that names none is the same for every part. Nothing has to cross between parts.
Inputs may be any that keep to these rules, and one draw needn't show every extreme that they name: `live_cols`: every patch has at least 8 live columns; some patch has all 32 columns live. `neighbours`: Entry t of a live slot at column c and latitude l names either the slot itself (extended index 256 + s) or the slot at column c + dc and latitude l + dl, with (dc, dl) = (-1,-1), (-1,0), (-1,1), (0,-1), (0,1), (1,-1), (1,0), (1,1) for t = 0 to 7; column -1 means the last live column of the previous patch and column live_cols[p] the first column of the next patch, and the latitude stays within 0 to 255. Dead slots name only themselves.
All inputs are finite; a program needn't handle non-finite values.
Results may differ from a plain program's by a relative error of at most 0.0039.
Values may be sent and summed in bfloat16 or wider, within the bound.
No kernel may reach another device: no remote copies, remote signals or barrier semaphores. Data moves between devices by JAX's collectives and lax.ppermute only.
A program may use at most 64 MiB of HBM per device.

v0:
```python
import jax
import jax.numpy as jnp
from jax import lax
from jax.sharding import PartitionSpec as P

DEG = 6
LATS = 256


tap_offsets = [(-1, -1), (-1, 0), (-1, 1), (0, -1), (0, 1), (1, -1), (1, 0), (1, 1)]


def shifted(value, axis, steps):
    count = lax.axis_size(axis)
    pairs = [(source, (source + steps) % count) for source in range(count)]
    return lax.ppermute(value, axis, pairs)


def tap_sum(padded, present, start, width):
    center = lax.slice_in_dim(padded, start, start + width, axis=1)
    summed = jnp.zeros(center.shape, jnp.float32)
    for tap_index in range(8):
        step_col, step_lat = tap_offsets[tap_index]
        moved_start = start + step_col * LATS + step_lat
        moved = lax.slice_in_dim(padded, moved_start, moved_start + width, axis=1)
        summed = summed + jnp.where(present[tap_index][None, :], moved, center)
    return -0.125 * summed


def rim_step(field, present, live):
    first_col = field[:, :LATS]
    last_col = lax.dynamic_slice_in_dim(field, (live - 1) * LATS, LATS, 1)
    from_prev = shifted(last_col, ("pix", "sub"), 1)
    from_next = shifted(first_col, ("pix", "sub"), -1)
    margin = LATS + 1
    channels = field.shape[0]
    padded = jnp.concatenate(
        [
            jnp.zeros((channels, margin), jnp.float32),
            from_prev,
            field,
            jnp.zeros((channels, LATS + margin), jnp.float32),
        ],
        axis=1,
    )
    padded = lax.dynamic_update_slice_in_dim(padded, from_next, margin + LATS + live * LATS, 1)
    return tap_sum(padded, present, margin + LATS, field.shape[1])


def shards(features, neighbours, live_cols, cheb_weight, out_bias):
    slot_count = features.shape[1]
    live = live_cols[0]
    own_slots = jnp.arange(slot_count, dtype=jnp.int32)[None, :]
    present = neighbours != LATS + own_slots
    terms = [features]
    older = features.astype(jnp.float32)
    newer = rim_step(older, present, live)
    terms.append(newer.astype(jnp.bfloat16))
    for degree in range(2, DEG + 1):
        upcoming = 2.0 * rim_step(newer, present, live) - older
        older, newer = (newer, upcoming)
        terms.append(newer.astype(jnp.bfloat16))
    share = slot_count // lax.axis_size("chan")
    summed = jnp.zeros((share, cheb_weight.shape[2]), jnp.float32)
    for degree in range(DEG + 1):
        piece = lax.all_to_all(terms[degree], "chan", split_axis=1, concat_axis=0, tiled=True)
        summed = summed + jnp.einsum(
            "ip,io->po", piece, cheb_weight[degree], preferred_element_type=jnp.float32
        )
    slots = lax.axis_index("chan") * share + jnp.arange(share, dtype=jnp.int32)
    alive = slots < live * LATS
    result = jnp.where(alive[:, None], summed + out_bias[None, :], 0.0)
    return result.astype(jnp.bfloat16).reshape(1, share, cheb_weight.shape[2])


def solution(mesh):
    in_specs = (
        P("chan", ("grp", "pix", "sub")),
        P(None, ("grp", "pix", "sub")),
        P(("grp", "pix", "sub")),
        P(),
        P(),
    )
    out_specs = P(("grp", "pix", "sub"), "chan", None)
    return jax.shard_map(shards, mesh=mesh, in_specs=in_specs, out_specs=out_specs, check_vma=False)
```

profile of v0, /device:TPU:0, one launch (start us, length us, event | category | flops | bytes accessed | tf_op | source)
XLA Modules:
  0.0 369.9 jit_solution(14855939197385692050)
XLA Ops:
  0.0 4.1 %copy.6 = bf16[128,8192]{0,1:T(8,128)(2,1)} copy(bf16[128,8192]{1,0:T(8,128)(2,1)} %param.5) | data formatting | bytes 4194304 | tf_op args[0]
  4.1 3.9 %convert_element_type.24 = f32[128,8192]{0,1:T(8,128)} convert(bf16[128,8192]{0,1:T(8,128)(2,1)} %copy.6) | non-fusion elementwise | flops 1048576 | bytes 6291456 | tf_op jit(solution)/shard_map/convert_element_type | solution.py:56
  10.9 4.1 %collective-permute-start.1 = (f32[128,256]{0,1:T(8,128)S(1)}, f32[128,256]{0,1:T(8,128)S(1)}, u32[]{:S(2)}, u32[]{:S(2)}) collective-permute-start(f32[128,256]{0,1:T(8,128)S(1)} %slice.341), channel_id=1, source_target_pairs={{0,13},{1,0},{4,1},{5,4},{8,5},{9,8},{12,9},{13,12},{2,15},{3,2},{... | collective-permute-start | bytes 393224 | tf_op jit(solution)/shard_map/ppermute | solution.py:16
  16.7 14.2 %concatenate.18 = f32[128,9218]{0,1:T(8,128)} concatenate(f32[128,257]{0,1:T(8,128)S(1)} %broadcast.29, f32[128,256]{0,1:T(8,128)S(1)} %collective-permute-done, bf16[128,8192]{0,1:T(8,128)(2,1)} %copy.6, f32[128,513]{0,1:T(8,128)S(1)} %broadcast.30), dimensions={1} | concatenate | bytes 7342080 | tf_op jit(solution)/shard_map/concatenate | solution.py:37
  32.6 20.4 %fusion.81 = (bf16[128,8192]{0,1:T(8,128)(2,1)}, f32[128,8192]{0,1:T(8,128)S(1)}) fusion(f32[128,9218]{0,1:T(8,128)} %dynamic_update_slice.18, pred[8192]{0:T(1024)(128)(4,1)S(1)} %get-tuple-element.6, pred[8192]{0:T(1024)(128)(4,1)S(1)} %get-tuple-element.7, pred[8192]{0:T(1024)(128)(4,1)S(1)} %get-tuple-element.8, ...), kind=kLoop, calls=%fused_computation.148 | loop fusion | flops 17825792 | bytes 44105728 | tf_op jit(solution)/shard_map/convert_element_type | solution.py:58
  53.0 2.1 copy-done.3
  55.2 3.5 collective-permute-start.3
  58.7 3.8 %all-to-all-start = ((bf16[128,2,4096]{0,2,1:T(8,128)(2,1)}), bf16[128,2,4096]{0,2,1:T(8,128)(2,1)S(1)}, u32[]{:S(2)}, u32[]{:S(2)}) async-start(bf16[128,2,4096]{0,2,1:T(8,128)(2,1)} %bitcast.1), calls=%async_computation | async-start | bytes 4194304 | tf_op jit(solution)/shard_map/all_to_all | solution.py:66
  62.5 14.5 %concatenate.19 = f32[128,9218]{0,1:T(8,128)} concatenate(f32[128,257]{0,1:T(8,128)S(1)} %broadcast.29, f32[128,256]{0,1:T(8,128)S(1)} %collective-permute-done.2, f32[128,8192]{0,1:T(8,128)} %copy-done.3, f32[128,513]{0,1:T(8,128)S(1)} %broadcast.30), dimensions={1} | concatenate | bytes 9439232 | tf_op jit(solution)/shard_map/concatenate | solution.py:37
  78.7 20.9 %fusion.79 = (bf16[128,8192]{0,1:T(8,128)(2,1)}, f32[128,8192]{0,1:T(8,128)S(1)}) fusion(bf16[128,8192]{0,1:T(8,128)(2,1)} %copy.6, f32[128,9218]{0,1:T(8,128)} %dynamic_update_slice.19, pred[8192]{0:T(1024)(128)(4,1)S(1)} %get-tuple-element.6, pred[8192]{0:T(1024)(128)(4,1)S(1)} %get-tuple-element.7, pred[8192]{0:T(1024)(128)(4,1)S(1)} %get-tuple-element.8, ...), kind=kLoop, calls=%fused_computation.147 | loop fusion | flops 19922944 | bytes 46202880 | tf_op jit(solution)/shard_map/convert_element_type | solution.py:62
  101.6 3.5 collective-permute-start.5
  105.1 3.0 collective-permute-done.4
  108.2 14.5 %concatenate.20 = f32[128,9218]{0,1:T(8,128)} concatenate(f32[128,257]{0,1:T(8,128)S(1)} %broadcast.29, f32[128,256]{0,1:T(8,128)S(1)} %collective-permute-done.4, f32[128,8192]{0,1:T(8,128)} %copy-done.2, f32[128,513]{0,1:T(8,128)S(1)} %broadcast.30), dimensions={1} | concatenate | bytes 9439232 | tf_op jit(solution)/shard_map/concatenate | solution.py:37
  124.4 4.8 %all-to-all-start.1 = ((bf16[128,2,4096]{0,2,1:T(8,128)(2,1)}), bf16[128,2,4096]{0,2,1:T(8,128)(2,1)}, u32[]{:S(2)}, u32[]{:S(2)}) async-start(bf16[128,2,4096]{0,2,1:T(8,128)(2,1)} %bitcast.64), calls=%async_computation.1 | async-start | bytes 4194304 | tf_op jit(solution)/shard_map/all_to_all | solution.py:66
  129.2 21.3 %fusion.77 = (bf16[128,8192]{0,1:T(8,128)(2,1)}, f32[128,8192]{0,1:T(8,128)S(1)}) fusion(f32[128,8192]{0,1:T(8,128)} %copy-done.3, f32[128,9218]{0,1:T(8,128)} %dynamic_update_slice.20, pred[8192]{0:T(1024)(128)(4,1)S(1)} %get-tuple-element.6, pred[8192]{0:T(1024)(128)(4,1)S(1)} %get-tuple-element.7, pred[8192]{0:T(1024)(128)(4,1)S(1)} %get-tuple-element.8, ...), kind=kLoop, calls=%fused_computation.146 | loop fusion | flops 18874368 | bytes 48300032 | tf_op jit(solution)/shard_map/convert_element_type | solution.py:62
  150.5 2.1 copy-done
  152.7 3.5 collective-permute-start.7
  156.2 2.6 collective-permute-done.6
  158.9 14.5 %concatenate.21 = f32[128,9218]{0,1:T(8,128)} concatenate(f32[128,257]{0,1:T(8,128)S(1)} %broadcast.29, f32[128,256]{0,1:T(8,128)S(1)} %collective-permute-done.6, f32[128,8192]{0,1:T(8,128)} %copy-done, f32[128,513]{0,1:T(8,128)S(1)} %broadcast.30), dimensions={1} | concatenate | bytes 9439232 | tf_op jit(solution)/shard_map/concatenate | solution.py:37
  175.0 3.8 %all-to-all-start.2 = ((bf16[128,2,4096]{0,2,1:T(8,128)(2,1)}), bf16[128,2,4096]{0,2,1:T(8,128)(2,1)S(1)}, u32[]{:S(2)}, u32[]{:S(2)}) async-start(bf16[128,2,4096]{0,2,1:T(8,128)(2,1)} %bitcast.10), calls=%async_computation.2 | async-start | bytes 4194304 | tf_op jit(solution)/shard_map/all_to_all | solution.py:66
  178.8 21.2 %fusion.75 = (bf16[128,8192]{0,1:T(8,128)(2,1)}, f32[128,8192]{0,1:T(8,128)S(1)}) fusion(f32[128,8192]{0,1:T(8,128)} %copy-done.2, f32[128,9218]{0,1:T(8,128)} %dynamic_update_slice.21, pred[8192]{0:T(1024)(128)(4,1)S(1)} %get-tuple-element.6, pred[8192]{0:T(1024)(128)(4,1)S(1)} %get-tuple-element.7, pred[8192]{0:T(1024)(128)(4,1)S(1)} %get-tuple-element.8, ...), kind=kLoop, calls=%fused_computation.145 | loop fusion | flops 18874368 | bytes 48300032 | tf_op jit(solution)/shard_map/convert_element_type | solution.py:62
  202.1 3.5 collective-permute-start.9
  205.6 2.6 collective-permute-done.8
  208.3 14.5 %concatenate.22 = f32[128,9218]{0,1:T(8,128)} concatenate(f32[128,257]{0,1:T(8,128)S(1)} %broadcast.29, f32[128,256]{0,1:T(8,128)S(1)} %collective-permute-done.8, f32[128,8192]{0,1:T(8,128)} %copy-done.1, f32[128,513]{0,1:T(8,128)S(1)} %broadcast.30), dimensions={1} | concatenate | bytes 9439232 | tf_op jit(solution)/shard_map/concatenate | solution.py:37
  224.4 4.8 %all-to-all-start.3 = ((bf16[128,2,4096]{0,2,1:T(8,128)(2,1)}), bf16[128,2,4096]{0,2,1:T(8,128)(2,1)}, u32[]{:S(2)}, u32[]{:S(2)}) async-start(bf16[128,2,4096]{0,2,1:T(8,128)(2,1)} %bitcast.14), calls=%async_computation.3 | async-start | bytes 4194304 | tf_op jit(solution)/shard_map/all_to_all | solution.py:66
  229.3 21.4 %fusion.73 = (bf16[128,8192]{0,1:T(8,128)(2,1)}, f32[128,8192]{0,1:T(8,128)S(1)}) fusion(f32[128,8192]{0,1:T(8,128)} %copy-done, f32[128,9218]{0,1:T(8,128)} %dynamic_update_slice.22, pred[8192]{0:T(1024)(128)(4,1)S(1)} %get-tuple-element.6, pred[8192]{0:T(1024)(128)(4,1)S(1)} %get-tuple-element.7, pred[8192]{0:T(1024)(128)(4,1)S(1)} %get-tuple-element.8, ...), kind=kLoop, calls=%fused_computation.144 | loop fusion | flops 18874368 | bytes 48300032 | tf_op jit(solution)/shard_map/convert_element_type | solution.py:62
  250.7 2.1 copy-done.4
  252.8 3.5 collective-permute-start.11
  256.3 2.6 collective-permute-done.10
  259.0 14.5 %concatenate.23 = f32[128,9218]{0,1:T(8,128)} concatenate(f32[128,257]{0,1:T(8,128)S(1)} %broadcast.29, f32[128,256]{0,1:T(8,128)S(1)} %collective-permute-done.10, f32[128,8192]{0,1:T(8,128)} %copy-done.4, f32[128,513]{0,1:T(8,128)S(1)} %broadcast.30), dimensions={1} | concatenate | bytes 9439232 | tf_op jit(solution)/shard_map/concatenate | solution.py:37
  275.2 4.8 %all-to-all-start.4 = ((bf16[128,2,4096]{0,2,1:T(8,128)(2,1)}), bf16[128,2,4096]{0,2,1:T(8,128)(2,1)}, u32[]{:S(2)}, u32[]{:S(2)}) async-start(bf16[128,2,4096]{0,2,1:T(8,128)(2,1)} %bitcast.18), calls=%async_computation.4 | async-start | bytes 4194304 | tf_op jit(solution)/shard_map/all_to_all | solution.py:66
  279.9 21.2 %fusion.7 = bf16[128,8192]{0,1:T(8,128)(2,1)} fusion(f32[128,8192]{0,1:T(8,128)} %copy-done.1, f32[128,9218]{0,1:T(8,128)} %dynamic_update_slice.23, pred[8192]{0:T(1024)(128)(4,1)S(1)} %get-tuple-element.6, pred[8192]{0:T(1024)(128)(4,1)S(1)} %get-tuple-element.7, pred[8192]{0:T(1024)(128)(4,1)S(1)} %get-tuple-element.8, ...), kind=kLoop, calls=%fused_computation.14 | loop fusion | flops 18874368 | bytes 44105728 | tf_op jit(solution)/shard_map/convert_element_type | solution.py:62
  301.2 3.0 copy.7
  304.2 5.0 %all-to-all-start.5 = ((bf16[128,2,4096]{0,2,1:T(8,128)(2,1)}), bf16[128,2,4096]{0,2,1:T(8,128)(2,1)}, u32[]{:S(2)}, u32[]{:S(2)}) async-start(bf16[128,2,4096]{0,2,1:T(8,128)(2,1)} %bitcast.54), calls=%async_computation.5 | async-start | bytes 4194304 | tf_op jit(solution)/shard_map/all_to_all | solution.py:66
  309.2 2.7 fusion.64
  311.9 4.1 %copy.9 = bf16[2,128,4096]{2,1,0:T(8,128)(2,1)} copy(bf16[2,128,4096]{1,2,0:T(8,128)(2,1)} %bitcast.7) | data formatting | bytes 4194304 | tf_op jit(solution)/shard_map/all_to_all | solution.py:66
  316.0 5.7 %convolution_add_fusion.5 = f32[4096,256]{1,0:T(8,128)} fusion(f32[4096,256]{1,0:T(8,128)} %fusion.64, bf16[256,4096]{1,0:T(8,128)(2,1)} %bitcast.60, bf16[7,256,256]{2,1,0:T(8,128)(2,1)S(1)} %copy-done.8), kind=kOutput, calls=%fused_computation.7 | convolution fusion | flops 537919488 | bytes 10616832 | tf_op jit(solution)/shard_map/ip,io->po/dot_general | solution.py:67
  321.7 2.7 copy.10
  324.4 5.5 %convolution_add_fusion.4 = f32[4096,256]{1,0:T(8,128)} fusion(f32[4096,256]{1,0:T(8,128)} %convolution_add_fusion.5, bf16[256,4096]{1,0:T(8,128)(2,1)} %bitcast.61, bf16[7,256,256]{2,1,0:T(8,128)(2,1)S(1)} %copy-done.8), kind=kOutput, calls=%fused_computation.6 | convolution fusion | flops 537919488 | bytes 10616832 | tf_op jit(solution)/shard_map/ip,io->po/dot_general | solution.py:67
  329.9 4.1 %copy.11 = bf16[2,128,4096]{2,1,0:T(8,128)(2,1)} copy(bf16[2,128,4096]{1,2,0:T(8,128)(2,1)} %bitcast.15) | data formatting | bytes 4194304 | tf_op jit(solution)/shard_map/all_to_all | solution.py:66
  334.0 3.8 %all-to-all-start.6 = ((bf16[128,2,4096]{0,2,1:T(8,128)(2,1)}), bf16[128,2,4096]{0,2,1:T(8,128)(2,1)S(1)}, u32[]{:S(2)}, u32[]{:S(2)}) async-start(bf16[128,2,4096]{0,2,1:T(8,128)(2,1)} %bitcast.65), calls=%async_computation.6 | async-start | bytes 4194304 | tf_op jit(solution)/shard_map/all_to_all | solution.py:66
  337.8 5.6 %convolution_add_fusion.3 = f32[4096,256]{1,0:T(8,128)} fusion(f32[4096,256]{1,0:T(8,128)} %convolution_add_fusion.4, bf16[256,4096]{1,0:T(8,128)(2,1)} %bitcast.58, bf16[7,256,256]{2,1,0:T(8,128)(2,1)S(1)} %copy-done.8), kind=kOutput, calls=%fused_computation.5 | convolution fusion | flops 537919488 | bytes 10616832 | tf_op jit(solution)/shard_map/ip,io->po/dot_general | solution.py:67
  343.3 4.1 %copy.12 = bf16[2,128,4096]{2,1,0:T(8,128)(2,1)} copy(bf16[2,128,4096]{1,2,0:T(8,128)(2,1)} %bitcast.19) | data formatting | bytes 4194304 | tf_op jit(solution)/shard_map/all_to_all | solution.py:66
  347.4 5.5 %convolution_add_fusion.2 = f32[4096,256]{1,0:T(8,128)} fusion(f32[4096,256]{1,0:T(8,128)} %convolution_add_fusion.3, bf16[256,4096]{1,0:T(8,128)(2,1)} %bitcast.62, bf16[7,256,256]{2,1,0:T(8,128)(2,1)S(1)} %copy-done.8), kind=kOutput, calls=%fused_computation.4 | convolution fusion | flops 537919488 | bytes 10616832 | tf_op jit(solution)/shard_map/ip,io->po/dot_general | solution.py:67
  352.9 4.1 %copy.13 = bf16[2,128,4096]{2,1,0:T(8,128)(2,1)} copy(bf16[2,128,4096]{1,2,0:T(8,128)(2,1)} %bitcast.23) | data formatting | bytes 4194304 | tf_op jit(solution)/shard_map/all_to_all | solution.py:66
  357.0 5.5 %convolution_add_fusion.1 = f32[4096,256]{1,0:T(8,128)} fusion(f32[4096,256]{1,0:T(8,128)} %convolution_add_fusion.2, bf16[256,4096]{1,0:T(8,128)(2,1)} %bitcast.63, bf16[7,256,256]{2,1,0:T(8,128)(2,1)S(1)} %copy-done.8), kind=kOutput, calls=%fused_computation.3 | convolution fusion | flops 537919488 | bytes 10616832 | tf_op jit(solution)/shard_map/ip,io->po/dot_general | solution.py:67
  362.6 2.8 copy.14
  365.4 4.5 %fusion.3 = bf16[1,4096,256]{2,1,0:T(8,128)(2,1)} fusion(f32[4096,256]{1,0:T(8,128)} %convolution_add_fusion.1, bf16[256,4096]{1,0:T(8,128)(2,1)} %bitcast.59, f32[256]{0:T(256)S(1)} %copy-done.10, pred[4096]{0:T(1024)(128)(4,1)S(1)} %add_compare_fusion, bf16[7,256,256]{2,1,0:T(8,128)(2,1)S(1)} %copy-done.8), kind=kOutput, calls=%fused_computation.9 | convolution fusion | flops 541065216 | bytes 8524800 | tf_op jit(solution)/shard_map/ip,io->po/dot_general | solution.py:67
  (59 shorter events, 18.5 us)
Async XLA Ops:
  4.1 10.9 %copy-start.9 = (s32[8,8192]{1,0:T(8,128)S(1)}, s32[8,8192]{1,0:T(8,128)}, u32[]{:S(2)}) copy-start(s32[8,8192]{1,0:T(8,128)} %param.6) | copy-start | bytes 786436
  9.5 7.2 %collective-permute-start = (f32[128,256]{0,1:T(8,128)S(1)}, f32[128,256]{0,1:T(8,128)S(1)}, u32[]{:S(2)}, u32[]{:S(2)}) collective-permute-start(f32[128,256]{0,1:T(8,128)S(1)} %constant_dynamic-slice_fusion.5), channel_id=1, source_target_pairs={{0,1},{1,4},{4,5},{5,8},{8,9},{9,12},{12,13},{13,0},{2,3},{3,6},{6... | collective-permute-start | bytes 393224 | tf_op jit(solution)/shard_map/ppermute | solution.py:16
  10.9 20.1 %collective-permute-start.1 = (f32[128,256]{0,1:T(8,128)S(1)}, f32[128,256]{0,1:T(8,128)S(1)}, u32[]{:S(2)}, u32[]{:S(2)}) collective-permute-start(f32[128,256]{0,1:T(8,128)S(1)} %slice.341), channel_id=1, source_target_pairs={{0,13},{1,0},{4,1},{5,4},{8,5},{9,8},{12,9},{13,12},{2,15},{3,2},{... | collective-permute-start | bytes 393224 | tf_op jit(solution)/shard_map/ppermute | solution.py:16
  53.0 2.1 copy-start.3
  55.1 7.4 %collective-permute-start.2 = (f32[128,256]{0,1:T(8,128)S(1)}, f32[128,256]{0,1:T(8,128)S(1)}, u32[]{:S(2)}, u32[]{:S(2)}) collective-permute-start(f32[128,256]{0,1:T(8,128)S(1)} %get-tuple-element.32), channel_id=1, source_target_pairs={{0,1},{1,4},{4,5},{5,8},{8,9},{9,12},{12,13},{13,0},{2,3},{3,6},{6... | collective-permute-start | bytes 393224 | tf_op jit(solution)/shard_map/ppermute | solution.py:16
  55.2 21.8 %collective-permute-start.3 = (f32[128,256]{0,1:T(8,128)S(1)}, f32[128,256]{0,1:T(8,128)S(1)}, u32[]{:S(2)}, u32[]{:S(2)}) collective-permute-start(f32[128,256]{0,1:T(8,128)S(1)} %get-tuple-element.31), channel_id=1, source_target_pairs={{0,13},{1,0},{4,1},{5,4},{8,5},{9,8},{12,9},{13,12},{2,15},{3,2},{... | collective-permute-start | bytes 393224 | tf_op jit(solution)/shard_map/ppermute | solution.py:16
  58.7 65.6 %all-to-all-start = ((bf16[128,2,4096]{0,2,1:T(8,128)(2,1)}), bf16[128,2,4096]{0,2,1:T(8,128)(2,1)S(1)}, u32[]{:S(2)}, u32[]{:S(2)}) async-start(bf16[128,2,4096]{0,2,1:T(8,128)(2,1)} %bitcast.1), calls=%async_computation | async-start | bytes 4194304 | tf_op jit(solution)/shard_map/all_to_all | solution.py:66
  99.5 2.0 copy-start.2
  101.5 6.6 %collective-permute-start.4 = (f32[128,256]{0,1:T(8,128)S(1)}, f32[128,256]{0,1:T(8,128)S(1)}, u32[]{:S(2)}, u32[]{:S(2)}) collective-permute-start(f32[128,256]{0,1:T(8,128)S(1)} %get-tuple-element.30), channel_id=1, source_target_pairs={{0,1},{1,4},{4,5},{5,8},{8,9},{9,12},{12,13},{13,0},{2,3},{3,6},{6... | collective-permute-start | bytes 393224 | tf_op jit(solution)/shard_map/ppermute | solution.py:16
  101.6 21.1 %collective-permute-start.5 = (f32[128,256]{0,1:T(8,128)S(1)}, f32[128,256]{0,1:T(8,128)S(1)}, u32[]{:S(2)}, u32[]{:S(2)}) collective-permute-start(f32[128,256]{0,1:T(8,128)S(1)} %get-tuple-element.29), channel_id=1, source_target_pairs={{0,13},{1,0},{4,1},{5,4},{8,5},{9,8},{12,9},{13,12},{2,15},{3,2},{... | collective-permute-start | bytes 393224 | tf_op jit(solution)/shard_map/ppermute | solution.py:16
  124.3 26.2 %copy-start.5 = (bf16[128,2,4096]{0,2,1:T(8,128)(2,1)}, bf16[128,2,4096]{0,2,1:T(8,128)(2,1)S(1)}, u32[]{:S(2)}) copy-start(bf16[128,2,4096]{0,2,1:T(8,128)(2,1)S(1)} %all-to-all-done) | copy-start | bytes 6291460
  124.4 50.7 %all-to-all-start.1 = ((bf16[128,2,4096]{0,2,1:T(8,128)(2,1)}), bf16[128,2,4096]{0,2,1:T(8,128)(2,1)}, u32[]{:S(2)}, u32[]{:S(2)}) async-start(bf16[128,2,4096]{0,2,1:T(8,128)(2,1)} %bitcast.64), calls=%async_computation.1 | async-start | bytes 4194304 | tf_op jit(solution)/shard_map/all_to_all | solution.py:66
  150.5 2.1 copy-start
  152.6 6.2 %collective-permute-start.6 = (f32[128,256]{0,1:T(8,128)S(1)}, f32[128,256]{0,1:T(8,128)S(1)}, u32[]{:S(2)}, u32[]{:S(2)}) collective-permute-start(f32[128,256]{0,1:T(8,128)S(1)} %get-tuple-element.28), channel_id=1, source_target_pairs={{0,1},{1,4},{4,5},{5,8},{8,9},{9,12},{12,13},{13,0},{2,3},{3,6},{6... | collective-permute-start | bytes 393224 | tf_op jit(solution)/shard_map/ppermute | solution.py:16
  152.7 20.7 %collective-permute-start.7 = (f32[128,256]{0,1:T(8,128)S(1)}, f32[128,256]{0,1:T(8,128)S(1)}, u32[]{:S(2)}, u32[]{:S(2)}) collective-permute-start(f32[128,256]{0,1:T(8,128)S(1)} %get-tuple-element.27), channel_id=1, source_target_pairs={{0,13},{1,0},{4,1},{5,4},{8,5},{9,8},{12,9},{13,12},{2,15},{3,2},{... | collective-permute-start | bytes 393224 | tf_op jit(solution)/shard_map/ppermute | solution.py:16
  175.0 49.4 %all-to-all-start.2 = ((bf16[128,2,4096]{0,2,1:T(8,128)(2,1)}), bf16[128,2,4096]{0,2,1:T(8,128)(2,1)S(1)}, u32[]{:S(2)}, u32[]{:S(2)}) async-start(bf16[128,2,4096]{0,2,1:T(8,128)(2,1)} %bitcast.10), calls=%async_computation.2 | async-start | bytes 4194304 | tf_op jit(solution)/shard_map/all_to_all | solution.py:66
  200.0 2.0 copy-start.1
  202.0 6.2 %collective-permute-start.8 = (f32[128,256]{0,1:T(8,128)S(1)}, f32[128,256]{0,1:T(8,128)S(1)}, u32[]{:S(2)}, u32[]{:S(2)}) collective-permute-start(f32[128,256]{0,1:T(8,128)S(1)} %get-tuple-element.26), channel_id=1, source_target_pairs={{0,1},{1,4},{4,5},{5,8},{8,9},{9,12},{12,13},{13,0},{2,3},{3,6},{6... | collective-permute-start | bytes 393224 | tf_op jit(solution)/shard_map/ppermute | solution.py:16
  202.1 20.7 %collective-permute-start.9 = (f32[128,256]{0,1:T(8,128)S(1)}, f32[128,256]{0,1:T(8,128)S(1)}, u32[]{:S(2)}, u32[]{:S(2)}) collective-permute-start(f32[128,256]{0,1:T(8,128)S(1)} %get-tuple-element.25), channel_id=1, source_target_pairs={{0,13},{1,0},{4,1},{5,4},{8,5},{9,8},{12,9},{13,12},{2,15},{3,2},{... | collective-permute-start | bytes 393224 | tf_op jit(solution)/shard_map/ppermute | solution.py:16
  224.4 26.2 %copy-start.6 = (bf16[128,2,4096]{0,2,1:T(8,128)(2,1)}, bf16[128,2,4096]{0,2,1:T(8,128)(2,1)S(1)}, u32[]{:S(2)}) copy-start(bf16[128,2,4096]{0,2,1:T(8,128)(2,1)S(1)} %all-to-all-done.2) | copy-start | bytes 6291460
  224.4 50.7 %all-to-all-start.3 = ((bf16[128,2,4096]{0,2,1:T(8,128)(2,1)}), bf16[128,2,4096]{0,2,1:T(8,128)(2,1)}, u32[]{:S(2)}, u32[]{:S(2)}) async-start(bf16[128,2,4096]{0,2,1:T(8,128)(2,1)} %bitcast.14), calls=%async_computation.3 | async-start | bytes 4194304 | tf_op jit(solution)/shard_map/all_to_all | solution.py:66
  250.7 2.1 copy-start.4
  252.7 6.2 %collective-permute-start.10 = (f32[128,256]{0,1:T(8,128)S(1)}, f32[128,256]{0,1:T(8,128)S(1)}, u32[]{:S(2)}, u32[]{:S(2)}) collective-permute-start(f32[128,256]{0,1:T(8,128)S(1)} %get-tuple-element.24), channel_id=1, source_target_pairs={{0,1},{1,4},{4,5},{5,8},{8,9},{9,12},{12,13},{13,0},{2,3},{3,6},{6... | collective-permute-start | bytes 393224 | tf_op jit(solution)/shard_map/ppermute | solution.py:16
  252.8 20.7 %collective-permute-start.11 = (f32[128,256]{0,1:T(8,128)S(1)}, f32[128,256]{0,1:T(8,128)S(1)}, u32[]{:S(2)}, u32[]{:S(2)}) collective-permute-start(f32[128,256]{0,1:T(8,128)S(1)} %get-tuple-element.23), channel_id=1, source_target_pairs={{0,13},{1,0},{4,1},{5,4},{8,5},{9,8},{12,9},{13,12},{2,15},{3,2},{... | collective-permute-start | bytes 393224 | tf_op jit(solution)/shard_map/ppermute | solution.py:16
  275.2 29.0 %all-to-all-start.4 = ((bf16[128,2,4096]{0,2,1:T(8,128)(2,1)}), bf16[128,2,4096]{0,2,1:T(8,128)(2,1)}, u32[]{:S(2)}, u32[]{:S(2)}) async-start(bf16[128,2,4096]{0,2,1:T(8,128)(2,1)} %bitcast.18), calls=%async_computation.4 | async-start | bytes 4194304 | tf_op jit(solution)/shard_map/all_to_all | solution.py:66
  301.1 8.0 %copy-start.8 = (bf16[7,256,256]{2,1,0:T(8,128)(2,1)S(1)}, bf16[7,256,256]{2,1,0:T(8,128)(2,1)}, u32[]{:S(2)}) copy-start(bf16[7,256,256]{2,1,0:T(8,128)(2,1)} %param.8) | copy-start | bytes 2752516
  304.2 29.8 %all-to-all-start.5 = ((bf16[128,2,4096]{0,2,1:T(8,128)(2,1)}), bf16[128,2,4096]{0,2,1:T(8,128)(2,1)}, u32[]{:S(2)}, u32[]{:S(2)}) async-start(bf16[128,2,4096]{0,2,1:T(8,128)(2,1)} %bitcast.54), calls=%async_computation.5 | async-start | bytes 4194304 | tf_op jit(solution)/shard_map/all_to_all | solution.py:66
  316.0 5.7 %copy-start.7 = (bf16[128,2,4096]{0,2,1:T(8,128)(2,1)S(1)}, bf16[128,2,4096]{0,2,1:T(8,128)(2,1)}, u32[]{:S(2)}) copy-start(bf16[128,2,4096]{0,2,1:T(8,128)(2,1)} %copy-done.6) | copy-start | bytes 6291460
  334.0 28.6 %all-to-all-start.6 = ((bf16[128,2,4096]{0,2,1:T(8,128)(2,1)}), bf16[128,2,4096]{0,2,1:T(8,128)(2,1)S(1)}, u32[]{:S(2)}, u32[]{:S(2)}) async-start(bf16[128,2,4096]{0,2,1:T(8,128)(2,1)} %bitcast.65), calls=%async_computation.6 | async-start | bytes 4194304 | tf_op jit(solution)/shard_map/all_to_all | solution.py:66
  362.6 2.8 copy-start.10
where the time goes:
time: 373 us; the launch traced here: 370 us
  local copies, waits for them, and re-layouts  138 us (37%)
  other arithmetic  130 us (35%)
  starting transfers between devices  53.3 us (14%)
  matrix products  35.1 us (9%)
  waiting for transfers between devices  12 us (3%)
    convert_element_type x6, other arithmetic, shards(): terms.append(newer.astype(jnp.bfloat16))  126 us
    concatenate x6, local copies, waits for them, and re-layouts, rim_step(): jnp.concatenate([jnp.zeros((channels, margin), jnp.float32), from_prev, f...  86.6 us
    dot_general x7, matrix products, shards(): jnp.einsum('ip,io->po', piece, cheb_weight[degree], preferred_element_typ...  35.1 us
    all_to_all x7, starting transfers between devices, shards(): lax.all_to_all(terms[degree], 'chan', split_axis=1, concat_axis=0, tiled=...  30.7 us
    all_to_all x7, local copies, waits for them, and re-layouts, shards(): lax.all_to_all(terms[degree], 'chan', split_axis=1, concat_axis=0, tiled=...  24.8 us
    ppermute x12, starting transfers between devices, shifted(): return lax.ppermute(value, axis, pairs)  22.6 us
    unnamed x23, local copies, waits for them, and re-layouts  14.2 us
    ppermute x12, waiting for transfers between devices, shifted(): return lax.ppermute(value, axis, pairs)  12 us
  transfers between devices with their start and end apart: 19, of which 5 were waited for; matrix products, arithmetic and copies ran while one was open for 69% of the time, Pallas kernels for 0%

commit v1 on v0

v1 whole, which is shorter than its diff:
```python
import functools

import jax
import jax.numpy as jnp
from jax import lax
from jax.experimental import pallas as pl
from jax.experimental.pallas import tpu as pltpu
from jax.sharding import PartitionSpec as P

DEG = 6
LATS = 256
HALF = LATS // 2
TAPS = 8
TAP_ROWS = 16


def shifted(value, axis, steps):
    count = lax.axis_size(axis)
    pairs = [(source, (source + steps) % count) for source in range(count)]
    return lax.ppermute(value, axis, pairs)


def sorting():
    latitude = lax.broadcasted_iota(jnp.int32, (LATS, LATS), 0)
    lane = lax.broadcasted_iota(jnp.int32, (LATS, LATS), 1)
    home = jnp.where(lane < HALF, 2 * lane, 2 * lane - (LATS - 1))
    return (latitude == home).astype(jnp.float32).astype(jnp.bfloat16)


def pack_kernel(columns, features, neighbours, out):
    channels = features.shape[0]
    sort = sorting()
    start = pl.program_id(0) * columns * LATS
    slots = LATS + start + lax.broadcasted_iota(jnp.int32, (TAPS, columns * LATS), 1)
    present = jnp.where(neighbours[...] != slots, 1.0, 0.0).astype(jnp.bfloat16)
    for column in range(columns):
        lanes = slice(column * LATS, (column + 1) * LATS)
        moved = jnp.dot(features[:, lanes], sort, preferred_element_type=jnp.float32)
        out[column, :channels] = moved.astype(jnp.bfloat16)
        taps = jnp.dot(present[:, lanes], sort, preferred_element_type=jnp.float32)
        out[column, channels:] = jnp.concatenate([taps, jnp.zeros_like(taps)], axis=0).astype(jnp.bfloat16)


def pack(features, neighbours):
    channels, slot_count = features.shape
    span = slot_count // LATS
    columns = 4
    rows = channels + TAP_ROWS
    return pl.pallas_call(
        functools.partial(pack_kernel, columns),
        grid=(span // columns,),
        in_specs=[
            pl.BlockSpec((channels, columns * LATS), lambda i: (0, i)),
            pl.BlockSpec((TAPS, columns * LATS), lambda i: (0, i)),
        ],
        out_specs=pl.BlockSpec((columns, rows, LATS), lambda i: (i, 0, 0)),
        out_shape=jax.ShapeDtypeStruct((span, rows, LATS), jnp.bfloat16),
    )(features, neighbours)


def mask_kernel(width, place, interior, left, right, out):
    start = place[0]

    def body(source, target, column, carry):
        tap = source[column, 0:TAPS].astype(jnp.float32) * -0.25
        own = -2.0 - jnp.sum(tap, axis=0, keepdims=True)
        ahead = jnp.concatenate([pltpu.roll(tap[:, :HALF], HALF - 1, 1), tap[:, HALF:]], axis=1)
        behind = jnp.concatenate([tap[:, :HALF], pltpu.roll(tap[:, HALF:], 1, 1)], axis=1)
        for index in range(3):
            for row, part in ((0, ahead), (1, tap), (2, behind)):
                entry = 3 * index + row
                tap_index = entry if entry < 4 else entry - 1
                coefficient = own if entry == 4 else part[tap_index : tap_index + 1]
                out[target + column, entry] = jnp.broadcast_to(coefficient, (8, LATS))
        return carry

    lax.fori_loop(0, DEG, functools.partial(body, left, 0), 0)
    lax.fori_loop(0, width, functools.partial(body, interior, DEG), 0)
    lax.fori_loop(0, DEG, functools.partial(body, right, start), 0)


def divisor(count, limit):
    return max(d for d in range(1, count + 1) if count % d == 0 and d <= max(limit, 1))


def chunk_kernel(width, first, last, place, interior, left, right, masks, weight, *refs):
    if first:
        out, *fields, terms = refs
    elif last:
        acc, bias, out, *fields, terms = refs
    else:
        acc, out, *fields, terms = refs
    channels = interior.shape[1]
    window = width + 2 * DEG
    start = place[0]

    for source, count, target in ((left, DEG, 0), (interior, width, DEG), (right, DEG, start)):

        def load(column, carry):
            value = source[column]
            fields[0][target + column] = value.astype(jnp.float32)
            terms[target + column, 0:channels] = value
            return carry

        lax.fori_loop(0, count, load, 0)

    def combine(mask, at, side, values, source):
        lanes = slice(side * HALF, (side + 1) * HALF)
        other = slice(source * HALF, (source + 1) * HALF)
        return (
            mask[at][:, lanes] * values[0][:, other]
            + mask[3 + at][:, lanes] * values[1][:, other]
            + mask[6 + at][:, lanes] * values[2][:, other]
        )

    for level in range(1, DEG + 1):
        newer, older, upcoming = fields[(level - 1) % 3], fields[(level - 2) % 3], fields[level % 3]
        columns = window - 2 * level
        together = divisor(columns, 52 * 8 // channels)

        def step(index, carry):
            for member in range(together):
                column = level + index * together + member
                mask = [masks[column, entry] for entry in range(9)]
                for base in range(0, channels, 16):
                    halves = []
                    for row in (base, base + 8):
                        rows = slice(row, row + 8)
                        values = [newer[column - 1, rows], newer[column, rows], newer[column + 1, rows]]
                        even = (
                            combine(mask, 1, 0, values, 0)
                            + combine(mask, 2, 0, values, 1)
                            + pltpu.roll(combine(mask, 0, 0, values, 1), 1, 1)
                        )
                        odd = (
                            combine(mask, 1, 1, values, 1)
                            + combine(mask, 0, 1, values, 0)
                            + pltpu.roll(combine(mask, 2, 1, values, 0), HALF - 1, 1)
                        )
                        value = jnp.concatenate([even, odd], axis=1)
                        if level == 1:
                            value = 0.5 * value
                        else:
                            value = value - older[column, rows]
                        if level < DEG:
                            upcoming[column, rows] = value
                        halves.append(value)
                    at = level * channels + base
                    terms[column, at : at + 16] = jnp.concatenate(halves, axis=0).astype(jnp.bfloat16)
            return carry

        lax.fori_loop(0, columns // together, step, 0)

    sort = sorting() if last else None
    pair = divisor(width, 2)

    def mix(index, carry):
        for member in range(pair):
            column = index * pair + member
            product = jnp.dot(weight[...], terms[DEG + column], preferred_element_type=jnp.float32)
            if not first:
                product = product + acc[column]
            if last:
                alive = (column < place[1]).astype(jnp.float32)
                product = ((product + bias[...]) * alive).astype(out.dtype)
                product = lax.dot_general(
                    sort, product, (((1,), (1,)), ((), ())), preferred_element_type=jnp.float32
                ).astype(out.dtype)
            out[column] = product
        return carry

    lax.fori_loop(0, width // pair, mix, 0)


VMEM = pl.BlockSpec(memory_space=pltpu.VMEM)
SMEM = pl.BlockSpec(memory_space=pltpu.SMEM)


def mask_step(width, place, pieces):
    return pl.pallas_call(
        functools.partial(mask_kernel, width),
        out_shape=jax.ShapeDtypeStruct((width + 2 * DEG, 9, 8, LATS), jnp.float32),
        in_specs=[SMEM, VMEM, VMEM, VMEM],
        out_specs=VMEM,
    )(place, *pieces)


def chunk_step(width, place, pieces, masks, weight, acc, bias):
    channels = pieces[0].shape[1]
    outs = weight.shape[0]
    first, last = acc is None, bias is not None
    window = width + 2 * DEG
    operands = [place, *pieces, masks, weight]
    if not first:
        operands.append(acc)
    if last:
        operands.append(bias)
    return pl.pallas_call(
        functools.partial(chunk_kernel, width, first, last),
        out_shape=jax.ShapeDtypeStruct((width, LATS, outs), jnp.bfloat16 if last else jnp.float32),
        in_specs=[SMEM] + [VMEM] * (len(operands) - 1),
        out_specs=VMEM,
        scratch_shapes=[pltpu.VMEM((window, channels, LATS), jnp.float32)] * 3
        + [pltpu.VMEM((window, (DEG + 1) * channels, LATS), jnp.bfloat16)],
        compiler_params=pltpu.CompilerParams(vmem_limit_bytes=48 * 2**20),
    )(*operands)


def pick(options, index):
    chosen = options[0]
    for position in range(1, len(options)):
        chosen = jnp.where(index == position, options[position], chosen)
    return chosen


def splits(native):
    if native % 64:
        return [(0, native)]
    return [(0, native // 2), (native // 2, 3 * native // 4), (3 * native // 4, native)]


def shards(features, neighbours, live_cols, cheb_weight, out_bias):
    native, slot_count = features.shape
    span = slot_count // LATS
    count = lax.axis_size("chan")
    me = lax.axis_index("chan")
    width = span // count
    live = live_cols[0]
    packed = pack(features, neighbours)
    from_prev = shifted(lax.dynamic_slice_in_dim(packed, live - DEG, DEG, axis=0), ("pix", "sub"), 1)
    from_next = shifted(packed[:DEG], ("pix", "sub"), -1)

    def left_of(rows, target):
        options = []
        for position in range(count):
            edge = position * width
            if edge >= DEG:
                options.append(packed[edge - DEG : edge, rows])
            else:
                options.append(jnp.concatenate([from_prev[edge:, rows], packed[:edge, rows]], axis=0))
        return pick(options, target)

    def right_of(rows, target):
        options = []
        for position in range(count):
            edge = (position + 1) * width
            part = packed[edge : edge + DEG, rows]
            options.append(jnp.pad(part, ((0, 2 * DEG - part.shape[0]), (0, 0), (0, 0))))
        base = pick(options, target)
        kept = jnp.clip(live - (target + 1) * width, 0, DEG)
        return lax.dynamic_update_slice_in_dim(base, from_next[:, rows], kept, axis=0)[:DEG]

    def inside_of(rows, target):
        return lax.dynamic_slice_in_dim(packed[:, rows], target * width, width, axis=0)

    def pieces_of(rows, target):
        return inside_of(rows, target), left_of(rows, target), right_of(rows, target)

    live_here = live - me * width
    place = jnp.stack([DEG + jnp.clip(live_here, 0, width), live_here])
    weights = jnp.transpose(cheb_weight, (2, 0, 1))

    blocks = [(0, 0, native, pieces_of(slice(0, native), me))]
    for distance in range(1, count):
        target = lax.rem(me + distance, count)
        for low, high in splits(native):
            sent = pieces_of(slice(low, high), target)
            blocks.append((distance, low, high, tuple(shifted(piece, "chan", distance) for piece in sent)))

    masks = mask_step(width, place, pieces_of(slice(native, native + TAP_ROWS), me))
    acc = None
    for index, (distance, low, high, pieces) in enumerate(blocks):
        source = lax.rem(me - distance + count, count)
        weight = lax.dynamic_slice_in_dim(weights, source * native + low, high - low, axis=2)
        weight = weight.reshape(weights.shape[0], -1)
        bias = out_bias[:, None] if index == len(blocks) - 1 else None
        acc = chunk_step(width, place, pieces, masks, weight, acc, bias)
    return acc.reshape(1, width * LATS, acc.shape[2])


def solution(mesh):
    in_specs = (
        P("chan", ("grp", "pix", "sub")),
        P(None, ("grp", "pix", "sub")),
        P(("grp", "pix", "sub")),
        P(),
        P(),
    )
    out_specs = P(("grp", "pix", "sub"), "chan", None)
    return jax.shard_map(shards, mesh=mesh, in_specs=in_specs, out_specs=out_specs, check_vma=False)
```

time: 373 us -> 108 us (0.29)
  other arithmetic: 130 us -> 5.92 us
  local copies, waits for them, and re-layouts: 138 us -> 23.2 us
  Pallas kernels: 0 us -> 60.8 us
  starting transfers between devices: 53.3 us -> 12.7 us
  matrix products: 35.1 us -> 0 us
  waiting for transfers between devices: 12 us -> 4.24 us
    convert_element_type x7 -> x0, other arithmetic: 130 us -> none  [the longest x6 126 us: shards(): terms.append(newer.astype(jnp.bfloat16))]
    concatenate x6 -> x0, local copies, waits for them, and re-layouts: 86.6 us -> none  [rim_step(): jnp.concatenate([jnp.zeros((channels, margin), jnp.float32), from_prev, f...]
    pallas_call x0 -> x6, Pallas kernels: none -> 60.8 us  [the longest x4 49.7 us: chunk_step(): pl.pallas_call(functools.partial(chunk_kernel, width, first, last), out_s...]
    dot_general x7 -> x0, matrix products: 35.1 us -> none  [shards(): jnp.einsum('ip,io->po', piece, cheb_weight[degree], preferred_element_typ...]
    all_to_all x7 -> x0, starting transfers between devices: 30.7 us -> none  [shards(): lax.all_to_all(terms[degree], 'chan', split_axis=1, concat_axis=0, tiled=...]
    all_to_all x7 -> x0, local copies, waits for them, and re-layouts: 24.8 us -> none  [shards(): lax.all_to_all(terms[degree], 'chan', split_axis=1, concat_axis=0, tiled=...]
    unnamed x23 -> x24, local copies, waits for them, and re-layouts: 14.2 us -> 3.65 us
    ppermute x12 -> x11, starting transfers between devices: 22.6 us -> 12.7 us  [shifted(): return lax.ppermute(value, axis, pairs)]
  transfers between devices with their start and end apart: 19 -> 11, of which waited for: 5 -> 2; matrix products, arithmetic and copies ran while one was open for 69% -> 20% of each run, Pallas kernels for 0% -> 41%
where the time goes in v1:
time: 108 us
  Pallas kernels  60.8 us (56%)
  local copies, waits for them, and re-layouts  23.2 us (21%)
  starting transfers between devices  12.7 us (12%)
  other arithmetic  5.92 us (5%)
  waiting for transfers between devices  4.24 us (4%)
    pallas_call x4, Pallas kernels, chunk_step(): pl.pallas_call(functools.partial(chunk_kernel, width, first, last), out_s...  49.7 us
    ppermute x11, starting transfers between devices, shifted(): return lax.ppermute(value, axis, pairs)  12.7 us
    pallas_call x1, Pallas kernels, pack(): pl.pallas_call(functools.partial(pack_kernel, columns), grid=(span // col...  6.71 us
    dynamic_slice x5, local copies, waits for them, and re-layouts, inside_of(): lax.dynamic_slice_in_dim(packed[:, rows], target * width, width, axis=0)  6.33 us
    slice x6, local copies, waits for them, and re-layouts, inside_of(): packed[:, rows]  5.71 us
    pallas_call x1, Pallas kernels, mask_step(): pl.pallas_call(functools.partial(mask_kernel, width), out_shape=jax.Shape...  4.33 us
    ppermute x11, waiting for transfers between devices, shifted(): return lax.ppermute(value, axis, pairs)  4.24 us
    dynamic_update_slice x4, local copies, waits for them, and re-layouts, right_of(): lax.dynamic_update_slice_in_dim(base, from_next[:, rows], kept, axis=0)  3.76 us
  transfers between devices with their start and end apart: 11, of which 2 were waited for; matrix products, arithmetic and copies ran while one was open for 20% of the time, Pallas kernels for 41%

profile of v1, /device:TPU:0, one launch (start us, length us, event | category | flops | bytes accessed | tf_op | source)
XLA Modules:
  0.0 107.7 jit_solution(16522515852628554641)
XLA Ops:
  0.0 6.7 %shard_map.55 = bf16[32,144,256]{2,1,0:T(8,128)(2,1)} custom-call(bf16[128,8192]{1,0:T(8,128)(2,1)} %features.1, s32[8,8192]{1,0:T(8,128)} %neighbours.1), custom_call_target="tpu_custom_call" | custom-call | tf_op jit(solution)/shard_map/pallas_call | solution.py:49
  6.7 2.4 %fusion.2 = (bf16[32,32,256]{2,1,0:T(8,128)(2,1)}, bf16[32,32,256]{2,1,0:T(8,128)(2,1)}) fusion(bf16[32,144,256]{2,1,0:T(8,128)(2,1)} %shard_map.55), kind=kLoop, calls=%fused_computation.28 | loop fusion | bytes 2097152 | tf_op jit(solution)/shard_map/slice | solution.py:254
  9.1 1.8 %constant_dynamic-slice_fusion.9 = bf16[16,32,256]{2,1,0:T(8,128)(2,1)} fusion(bf16[32,32,256]{2,1,0:T(8,128)(2,1)} %get-tuple-element.14, s32[]{:T(128)S(6)} %select_n.101), kind=kLoop, calls=%fused_computation.24 | loop fusion | bytes 524292 | tf_op jit(solution)/shard_map/dynamic_slice | solution.py:254
  10.9 2.9 %collective-permute-start = (bf16[16,32,256]{2,1,0:T(8,128)(2,1)}, bf16[16,32,256]{2,1,0:T(8,128)(2,1)}, u32[]{:S(2)}, u32[]{:S(2)}) collective-permute-start(bf16[16,32,256]{2,1,0:T(8,128)(2,1)} %constant_dynamic-slice_fusion.9), channel_id=1, source_target_pairs={{0,2},{2,0},{1,3},{3,1},{4,6},{6,4},{5,7},{7,5},{8,10},{10,8},{9,1... | collective-permute-start | bytes 786440 | tf_op jit(solution)/shard_map/ppermute | solution.py:20
  14.5 1.0 fusion.4
  15.5 0.0 collective-permute-start.1
  15.5 3.5 %collective-permute-start.3 = (bf16[6,144,256]{2,1,0:T(8,128)(2,1)}, bf16[6,144,256]{2,1,0:T(8,128)(2,1)}, u32[]{:S(2)}, u32[]{:S(2)}) collective-permute-start(bf16[6,144,256]{2,1,0:T(8,128)(2,1)} %get-tuple-element.17), channel_id=1, source_target_pairs={{0,13},{1,0},{4,1},{5,4},{8,5},{9,8},{12,9},{13,12},{2,15},{3,2},{... | collective-permute-start | bytes 1327112 | tf_op jit(solution)/shard_map/ppermute | solution.py:20
  19.0 1.7 %constant_dynamic-slice_fusion.5 = bf16[16,32,256]{2,1,0:T(8,128)(2,1)} fusion(bf16[32,32,256]{2,1,0:T(8,128)(2,1)} %get-tuple-element.13, s32[]{:T(128)S(6)} %select_n.101), kind=kLoop, calls=%fused_computation.20 | loop fusion | bytes 524292 | tf_op jit(solution)/shard_map/dynamic_slice | solution.py:254
  20.7 0.0 collective-permute-start.5
  20.7 0.8 constant_dynamic-slice_fusion.3
  21.5 2.0 %collective-permute-start.8 = (bf16[16,64,256]{2,1,0:T(8,128)(2,1)}, bf16[16,64,256]{2,1,0:T(8,128)(2,1)S(1)}, u32[]{:S(2)}, u32[]{:S(2)}) collective-permute-start(bf16[16,64,256]{2,1,0:T(8,128)(2,1)} %constant_dynamic-slice_fusion.3), channel_id=1, source_target_pairs={{0,2},{2,0},{1,3},{3,1},{4,6},{6,4},{5,7},{7,5},{8,10},{10,8},{9,1... | collective-permute-start | bytes 1572872 | tf_op jit(solution)/shard_map/ppermute | solution.py:20
  23.6 3.2 %slice.149 = bf16[32,128,256]{2,1,0:T(8,128)(2,1)} slice(bf16[32,144,256]{2,1,0:T(8,128)(2,1)} %shard_map.55), slice={[0:32], [0:128], [0:256]} | slice | bytes 4194304 | tf_op jit(solution)/shard_map/slice | solution.py:254
  26.8 0.1 copy.13.weight
  26.9 0.1 copy.12.weight
  27.1 0.1 copy.11.weight
  27.2 0.2 copy.10.weight
  27.5 0.1 copy.14.refs_1_
  27.6 0.1 slice-done.1
  27.7 0.7 constant_dynamic-slice_fusion.7.interior
  28.4 1.4 %constant_dynamic-slice_fusion.1.interior = bf16[16,128,256]{2,1,0:T(8,128)(2,1)S(1)} fusion(bf16[32,128,256]{2,1,0:T(8,128)(2,1)} %slice.149, s32[]{:T(128)S(6)} %select_n.107), kind=kLoop, calls=%fused_computation.16 | loop fusion | bytes 2097156 | tf_op jit(solution)/shard_map/dynamic_slice | solution.py:254
  29.8 0.7 pad_add_fusion.place
  30.5 1.0 fusion.1
  31.4 0.1 collective-permute-start.9
  31.6 1.0 slice_dynamic-update-slice_fusion.1
  32.5 2.1 %collective-permute-start.10 = (bf16[6,64,256]{2,1,0:T(8,128)(2,1)S(1)}, bf16[6,64,256]{2,1,0:T(8,128)(2,1)S(1)}, u32[]{:S(2)}, u32[]{:S(2)}) collective-permute-start(bf16[6,64,256]{2,1,0:T(8,128)(2,1)S(1)} %slice.148), channel_id=1, source_target_pairs={{0,2},{2,0},{1,3},{3,1},{4,6},{6,4},{5,7},{7,5},{8,10},{10,8},{9,1... | collective-permute-start | bytes 589832 | tf_op jit(solution)/shard_map/ppermute | solution.py:20
  34.6 1.1 fusion
  35.7 0.1 pad_select_fusion
  35.7 1.7 %slice_select_fusion.2 = (bf16[6,32,256]{2,1,0:T(8,128)(2,1)}, bf16[6,32,256]{2,1,0:T(8,128)(2,1)}, bf16[6,32,256]{2,1,0:T(8,128)(2,1)S(1)}, bf16[6,32,256]{2,1,0:T(8,128)(2,1)S(1)}) fusion(bf16[6,144,256]{2,1,0:T(8,128)(2,1)} %collective-permute-done.1, bf16[32,144,256]{2,1,0:T(8,128)(2,1)S(1)} %copy-done.9, pred[]{:T(512)S(6)} %eq.4), kind=kLoop, calls=%fused_computation.9 | loop fusion | flops 98304 | bytes 983041 | tf_op jit(solution)/shard_map/jit(_where)/select_n | solution.py:212
  37.4 1.0 slice_dynamic-update-slice_fusion
  38.5 1.0 slice_dynamic-update-slice_fusion.2
  39.5 1.4 %fusion.3 = (bf16[6,16,256]{2,1,0:T(8,128)(2,1)S(1)}, bf16[6,16,256]{2,1,0:T(8,128)(2,1)}) fusion(bf16[32,144,256]{2,1,0:T(8,128)(2,1)S(1)} %copy-done.9, bf16[6,144,256]{2,1,0:T(8,128)(2,1)} %collective-permute-done.1, pred[]{:T(512)S(6)} %eq.5), kind=kLoop, calls=%fused_computation.29 | loop fusion | flops 24576 | bytes 245761 | tf_op jit(solution)/shard_map/slice | solution.py:247
  40.9 0.6 slice.130
  41.6 0.6 slice.142
  42.2 0.7 copy-done.1
  42.9 0.0 collective-permute-start.2
  42.9 2.0 %collective-permute-start.4 = (bf16[6,32,256]{2,1,0:T(8,128)(2,1)}, bf16[6,32,256]{2,1,0:T(8,128)(2,1)}, u32[]{:S(2)}, u32[]{:S(2)}) collective-permute-start(bf16[6,32,256]{2,1,0:T(8,128)(2,1)} %slice.130), channel_id=1, source_target_pairs={{0,2},{2,0},{1,3},{3,1},{4,6},{6,4},{5,7},{7,5},{8,10},{10,8},{9,1... | collective-permute-start | bytes 294920 | tf_op jit(solution)/shard_map/ppermute | solution.py:20
  44.9 0.7 collective-permute-done.9.left
  45.6 0.7 copy-done.3
  46.3 3.5 %collective-permute-done.10.right = bf16[6,64,256]{2,1,0:T(8,128)(2,1)S(1)} collective-permute-done((bf16[6,64,256]{2,1,0:T(8,128)(2,1)S(1)}, bf16[6,64,256]{2,1,0:T(8,128)(2,1)S(1)}, u32[]{:S(2)}, u32[]{:S(2)}) %collective-permute-start.10) | collective-permute-done | bytes 196640 | tf_op jit(solution)/shard_map/ppermute | solution.py:20
  49.8 0.7 copy-done.5
  50.5 0.8 slice_dynamic-update-slice_fusion.4
  51.3 0.6 slice.136.right
  52.0 4.3 %shard_map.56.masks = f32[28,9,8,256]{3,2,1,0:T(8,128)} custom-call(s32[2]{0:T(128)} %pad_add_fusion.place, bf16[16,16,256]{2,1,0:T(8,128)(2,1)} %constant_dynamic-slice_fusion.7.interior, bf16[6,16,256]{2,1,0:T(8,128)(2,1)} %get-tuple-element.16.left, bf16[6,16,256]{2,1,0:T(8,128)(2,1)} %slice.136.right), custom_call_target="tpu_custom_call" | custom-call | tf_op jit(solution)/shard_map/pallas_call | solution.py:180
  56.3 1.6 %copy-done = f32[28,9,8,256]{3,2,1,0:T(8,128)S(1)} copy-done((f32[28,9,8,256]{3,2,1,0:T(8,128)S(1)}, f32[28,9,8,256]{3,2,1,0:T(8,128)}, u32[]{:S(2)}) %copy-start) | copy-done | bytes 2064408
  57.9 17.2 %shard_map.57.refs_0_ = f32[16,256,256]{2,1,0:T(8,128)} custom-call(s32[2]{0:T(128)S(1)} %copy-done.7, bf16[16,128,256]{2,1,0:T(8,128)(2,1)S(1)} %constant_dynamic-slice_fusion.1.interior, bf16[6,128,256]{2,1,0:T(8,128)(2,1)S(1)} %get-tuple-element.8.left, bf16[6,128,256]{2,1,0:T(8,128)(2,1)S(1)} %slice.154.right, f32[28,9,8,256]{3,2,1,0:T(8,128)S(1)} %copy-done, ...), custom_call_target="tpu_custom_call" | custom-call | tf_op jit(solution)/shard_map/pallas_call | solution.py:198
  75.1 13.0 %shard_map.58.refs_0_ = f32[16,256,256]{2,1,0:T(8,128)} custom-call(s32[2]{0:T(128)S(1)} %copy-done.7, bf16[16,64,256]{2,1,0:T(8,128)(2,1)S(1)} %collective-permute-done.8.interior, bf16[6,64,256]{2,1,0:T(8,128)(2,1)S(1)} %copy-done.4, bf16[6,64,256]{2,1,0:T(8,128)(2,1)S(1)} %copy-done.6, f32[28,9,8,256]{3,2,1,0:T(8,128)S(1)} %copy-done, ...), custom_call_target="tpu_custom_call" | custom-call | tf_op jit(solution)/shard_map/pallas_call | solution.py:198
  88.1 9.1 %shard_map.59.refs_0_ = f32[16,256,256]{2,1,0:T(8,128)} custom-call(s32[2]{0:T(128)S(1)} %copy-done.7, bf16[16,32,256]{2,1,0:T(8,128)(2,1)S(1)} %copy-done.2, bf16[6,32,256]{2,1,0:T(8,128)(2,1)} %collective-permute-done.6.left, bf16[6,32,256]{2,1,0:T(8,128)(2,1)} %collective-permute-done.7.right, f32[28,9,8,256]{3,2,1,0:T(8,128)S(1)} %copy-done, ...), custom_call_target="tpu_custom_call" | custom-call | tf_op jit(solution)/shard_map/pallas_call | solution.py:198
  97.3 10.4 %shard_map.60 = bf16[16,256,256]{2,1,0:T(8,128)(2,1)} custom-call(s32[2]{0:T(128)S(1)} %copy-done.7, bf16[16,32,256]{2,1,0:T(8,128)(2,1)} %collective-permute-done.interior, bf16[6,32,256]{2,1,0:T(8,128)(2,1)} %collective-permute-done.2.left, bf16[6,32,256]{2,1,0:T(8,128)(2,1)} %collective-permute-done.4.right, f32[28,9,8,256]{3,2,1,0:T(8,128)S(1)} %copy-done, ...), custom_call_target="tpu_custom_call" | custom-call | tf_op jit(solution)/shard_map/pallas_call | solution.py:198
  (42 shorter events, 0.3 us)
Async XLA Ops:
  6.7 7.8 %copy-start.8 = (bf16[32,144,256]{2,1,0:T(8,128)(2,1)S(1)}, bf16[32,144,256]{2,1,0:T(8,128)(2,1)}, u32[]{:S(2)}) copy-start(bf16[32,144,256]{2,1,0:T(8,128)(2,1)} %shard_map.55) | copy-start | bytes 7077892
  9.1 11.6 %slice-start = ((bf16[32,144,256]{2,1,0:T(8,128)(2,1)}), bf16[32,64,256]{2,1,0:T(8,128)(2,1)S(1)}, s32[]{:S(2)}) async-start(bf16[32,144,256]{2,1,0:T(8,128)(2,1)} %shard_map.55), calls=%async_computation | async-start | bytes 2097152 | tf_op jit(solution)/shard_map/slice | solution.py:254
  10.9 86.4 %collective-permute-start = (bf16[16,32,256]{2,1,0:T(8,128)(2,1)}, bf16[16,32,256]{2,1,0:T(8,128)(2,1)}, u32[]{:S(2)}, u32[]{:S(2)}) collective-permute-start(bf16[16,32,256]{2,1,0:T(8,128)(2,1)} %constant_dynamic-slice_fusion.9), channel_id=1, source_target_pairs={{0,2},{2,0},{1,3},{3,1},{4,6},{6,4},{5,7},{7,5},{8,10},{10,8},{9,1... | collective-permute-start | bytes 786440 | tf_op jit(solution)/shard_map/ppermute | solution.py:20
  15.5 15.0 %collective-permute-start.1 = (bf16[6,144,256]{2,1,0:T(8,128)(2,1)}, bf16[6,144,256]{2,1,0:T(8,128)(2,1)}, u32[]{:S(2)}, u32[]{:S(2)}) collective-permute-start(bf16[6,144,256]{2,1,0:T(8,128)(2,1)} %get-tuple-element.18), channel_id=1, source_target_pairs={{0,1},{1,4},{4,5},{5,8},{8,9},{9,12},{12,13},{13,0},{2,3},{3,6},{6... | collective-permute-start | bytes 1327112 | tf_op jit(solution)/shard_map/ppermute | solution.py:20
  15.5 16.1 %collective-permute-start.3 = (bf16[6,144,256]{2,1,0:T(8,128)(2,1)}, bf16[6,144,256]{2,1,0:T(8,128)(2,1)}, u32[]{:S(2)}, u32[]{:S(2)}) collective-permute-start(bf16[6,144,256]{2,1,0:T(8,128)(2,1)} %get-tuple-element.17), channel_id=1, source_target_pairs={{0,13},{1,0},{4,1},{5,4},{8,5},{9,8},{12,9},{13,12},{2,15},{3,2},{... | collective-permute-start | bytes 1327112 | tf_op jit(solution)/shard_map/ppermute | solution.py:20
  20.7 21.5 %collective-permute-start.5 = (bf16[16,32,256]{2,1,0:T(8,128)(2,1)}, bf16[16,32,256]{2,1,0:T(8,128)(2,1)S(1)}, u32[]{:S(2)}, u32[]{:S(2)}) collective-permute-start(bf16[16,32,256]{2,1,0:T(8,128)(2,1)} %constant_dynamic-slice_fusion.5), channel_id=1, source_target_pairs={{0,2},{2,0},{1,3},{3,1},{4,6},{6,4},{5,7},{7,5},{8,10},{10,8},{9,1... | collective-permute-start | bytes 786440 | tf_op jit(solution)/shard_map/ppermute | solution.py:20
  21.5 21.4 %collective-permute-start.8 = (bf16[16,64,256]{2,1,0:T(8,128)(2,1)}, bf16[16,64,256]{2,1,0:T(8,128)(2,1)S(1)}, u32[]{:S(2)}, u32[]{:S(2)}) collective-permute-start(bf16[16,64,256]{2,1,0:T(8,128)(2,1)} %constant_dynamic-slice_fusion.3), channel_id=1, source_target_pairs={{0,2},{2,0},{1,3},{3,1},{4,6},{6,4},{5,7},{7,5},{8,10},{10,8},{9,1... | collective-permute-start | bytes 1572872 | tf_op jit(solution)/shard_map/ppermute | solution.py:20
  23.6 3.2 %copy-start.10 = (bf16[7,256,256]{2,1,0:T(8,128)(2,1)S(1)}, bf16[7,256,256]{2,1,0:T(8,128)(2,1)}, u32[]{:S(2)}) copy-start(bf16[7,256,256]{2,1,0:T(8,128)(2,1)} %param.8) | copy-start | bytes 2752516
  26.8 0.7 copy-start.11
  26.8 1.0 slice-start.1
  27.7 2.7 %copy-start.9 = (bf16[32,144,256]{2,1,0:T(8,128)(2,1)S(1)}, bf16[32,144,256]{2,1,0:T(8,128)(2,1)}, u32[]{:S(2)}) copy-start(bf16[32,144,256]{2,1,0:T(8,128)(2,1)} %shard_map.55) | copy-start | bytes 7077892
  31.4 14.2 %collective-permute-start.9 = (bf16[6,64,256]{2,1,0:T(8,128)(2,1)S(1)}, bf16[6,64,256]{2,1,0:T(8,128)(2,1)S(1)}, u32[]{:S(2)}, u32[]{:S(2)}) collective-permute-start(bf16[6,64,256]{2,1,0:T(8,128)(2,1)S(1)} %get-tuple-element.10), channel_id=1, source_target_pairs={{0,2},{2,0},{1,3},{3,1},{4,6},{6,4},{5,7},{7,5},{8,10},{10,8},{9,1... | collective-permute-start | bytes 589832 | tf_op jit(solution)/shard_map/ppermute | solution.py:20
  32.5 17.3 %collective-permute-start.10 = (bf16[6,64,256]{2,1,0:T(8,128)(2,1)S(1)}, bf16[6,64,256]{2,1,0:T(8,128)(2,1)S(1)}, u32[]{:S(2)}, u32[]{:S(2)}) collective-permute-start(bf16[6,64,256]{2,1,0:T(8,128)(2,1)S(1)} %slice.148), channel_id=1, source_target_pairs={{0,2},{2,0},{1,3},{3,1},{4,6},{6,4},{5,7},{7,5},{8,10},{10,8},{9,1... | collective-permute-start | bytes 589832 | tf_op jit(solution)/shard_map/ppermute | solution.py:20
  38.5 17.8 %copy-start.7 = (s32[2]{0:T(128)S(1)}, s32[2]{0:T(128)}, u32[]{:S(2)}) copy-start(s32[2]{0:T(128)} %pad_add_fusion.place) | copy-start | bytes 28
  42.2 0.7 copy-start.1
  42.9 54.4 %collective-permute-start.2 = (bf16[6,32,256]{2,1,0:T(8,128)(2,1)}, bf16[6,32,256]{2,1,0:T(8,128)(2,1)}, u32[]{:S(2)}, u32[]{:S(2)}) collective-permute-start(bf16[6,32,256]{2,1,0:T(8,128)(2,1)} %get-tuple-element.6), channel_id=1, source_target_pairs={{0,2},{2,0},{1,3},{3,1},{4,6},{6,4},{5,7},{7,5},{8,10},{10,8},{9,1... | collective-permute-start | bytes 294920 | tf_op jit(solution)/shard_map/ppermute | solution.py:20
  42.9 54.3 %collective-permute-start.4 = (bf16[6,32,256]{2,1,0:T(8,128)(2,1)}, bf16[6,32,256]{2,1,0:T(8,128)(2,1)}, u32[]{:S(2)}, u32[]{:S(2)}) collective-permute-start(bf16[6,32,256]{2,1,0:T(8,128)(2,1)} %slice.130), channel_id=1, source_target_pairs={{0,2},{2,0},{1,3},{3,1},{4,6},{6,4},{5,7},{7,5},{8,10},{10,8},{9,1... | collective-permute-start | bytes 294920 | tf_op jit(solution)/shard_map/ppermute | solution.py:20
  45.6 0.7 copy-start.3
  46.3 41.8 %collective-permute-start.6 = (bf16[6,32,256]{2,1,0:T(8,128)(2,1)}, bf16[6,32,256]{2,1,0:T(8,128)(2,1)}, u32[]{:S(2)}, u32[]{:S(2)}) collective-permute-start(bf16[6,32,256]{2,1,0:T(8,128)(2,1)} %get-tuple-element.5), channel_id=1, source_target_pairs={{0,2},{2,0},{1,3},{3,1},{4,6},{6,4},{5,7},{7,5},{8,10},{10,8},{9,1... | collective-permute-start | bytes 294920 | tf_op jit(solution)/shard_map/ppermute | solution.py:20
  49.8 0.7 copy-start.5
  50.5 37.6 %collective-permute-start.7 = (bf16[6,32,256]{2,1,0:T(8,128)(2,1)}, bf16[6,32,256]{2,1,0:T(8,128)(2,1)}, u32[]{:S(2)}, u32[]{:S(2)}) collective-permute-start(bf16[6,32,256]{2,1,0:T(8,128)(2,1)} %slice.142), channel_id=1, source_target_pairs={{0,2},{2,0},{1,3},{3,1},{4,6},{6,4},{5,7},{7,5},{8,10},{10,8},{9,1... | collective-permute-start | bytes 294920 | tf_op jit(solution)/shard_map/ppermute | solution.py:20
  56.3 1.6 %copy-start = (f32[28,9,8,256]{3,2,1,0:T(8,128)S(1)}, f32[28,9,8,256]{3,2,1,0:T(8,128)}, u32[]{:S(2)}) copy-start(f32[28,9,8,256]{3,2,1,0:T(8,128)} %shard_map.56.masks) | copy-start | bytes 6193156
  57.9 17.2 %copy-start.4 = (bf16[6,64,256]{2,1,0:T(8,128)(2,1)S(1)}, bf16[6,64,256]{2,1,0:T(8,128)(2,1)}, u32[]{:S(2)}) copy-start(bf16[6,64,256]{2,1,0:T(8,128)(2,1)} %copy-done.3) | copy-start | bytes 589828
  57.9 17.2 %copy-start.6 = (bf16[6,64,256]{2,1,0:T(8,128)(2,1)S(1)}, bf16[6,64,256]{2,1,0:T(8,128)(2,1)}, u32[]{:S(2)}) copy-start(bf16[6,64,256]{2,1,0:T(8,128)(2,1)} %copy-done.5) | copy-start | bytes 589828
  75.1 13.0 %copy-start.2 = (bf16[16,32,256]{2,1,0:T(8,128)(2,1)S(1)}, bf16[16,32,256]{2,1,0:T(8,128)(2,1)}, u32[]{:S(2)}) copy-start(bf16[16,32,256]{2,1,0:T(8,128)(2,1)} %copy-done.1) | copy-start | bytes 786436

commit v2 on v0

v2 whole, which is shorter than its diff:
```python
import functools

import jax
import jax.numpy as jnp
from jax import lax
from jax.experimental import pallas as pl
from jax.experimental.pallas import tpu as pltpu
from jax.sharding import PartitionSpec as P

DEG = 6
LATS = 256
HALF = LATS // 2
TAPS = 8
TAP_ROWS = 16


def shifted(value, axis, steps):
    count = lax.axis_size(axis)
    pairs = [(source, (source + steps) % count) for source in range(count)]
    return lax.ppermute(value, axis, pairs)


def sorting():
    latitude = lax.broadcasted_iota(jnp.int32, (LATS, LATS), 0)
    lane = lax.broadcasted_iota(jnp.int32, (LATS, LATS), 1)
    home = jnp.where(lane < HALF, 2 * lane, 2 * lane - (LATS - 1))
    return (latitude == home).astype(jnp.float32).astype(jnp.bfloat16)


VMEM = pl.BlockSpec(memory_space=pltpu.VMEM)
SMEM = pl.BlockSpec(memory_space=pltpu.SMEM)
ANY = pl.BlockSpec(memory_space=pl.ANY)


def pack_kernel(span, width, targets, groups, place, features, neighbours, *refs):
    packed, last, first, *early = refs[: 3 + targets]
    held, listed, present, moved, in_sems, out_sems, edge_sems = refs[3 + targets :]
    channels = features.shape[0]
    size = span // groups
    lanes = size * LATS
    lists = pltpu.make_async_copy(neighbours, listed, in_sems.at[groups])
    lists.start()
    loads = []
    for group in range(groups):
        part = pl.ds(group * lanes, lanes)
        loads.append(pltpu.make_async_copy(features.at[:, part], held.at[:, part], in_sems.at[group]))
        loads[-1].start()
    sort = sorting()
    lists.wait()
    slots = LATS + lax.broadcasted_iota(jnp.int32, listed.shape, 1)
    present[0:TAPS] = jnp.where(listed[...] != slots, 1.0, 0.0).astype(jnp.bfloat16)
    present[TAPS:] = jnp.zeros((TAP_ROWS - TAPS, listed.shape[1]), jnp.bfloat16)
    stores = []
    for group in range(groups):
        loads[group].wait()
        for column in range(group * size, (group + 1) * size):
            at = slice(column * LATS, (column + 1) * LATS)
            value = jnp.concatenate([held[:, at], present[:, at]], axis=0)
            moved[column] = jnp.dot(value, sort, preferred_element_type=jnp.float32).astype(jnp.bfloat16)
        part = pl.ds(group * size, size)
        stores.append(pltpu.make_async_copy(moved.at[part], packed.at[part], out_sems.at[group]))
        stores[-1].start()
    for index in range(targets):
        part = moved.at[pl.ds(place[1 + index], width), pl.ds(0, channels)]
        stores.append(pltpu.make_async_copy(part, early[index], edge_sems.at[2 + index]))
    stores.append(pltpu.make_async_copy(moved.at[pl.ds(place[0] - DEG, DEG)], last, edge_sems.at[0]))
    stores.append(pltpu.make_async_copy(moved.at[pl.ds(0, DEG)], first, edge_sems.at[1]))
    for store in stores[groups:]:
        store.start()
    for store in stores:
        store.wait()


def pack(features, neighbours, place, width, targets):
    channels, slot_count = features.shape
    span = slot_count // LATS
    rows = channels + TAP_ROWS
    groups = 4
    shapes = [(span, rows), (DEG, rows), (DEG, rows)] + [(width, channels)] * targets
    return pl.pallas_call(
        functools.partial(pack_kernel, span, width, targets, groups),
        in_specs=[SMEM, ANY, ANY],
        out_specs=[ANY] * len(shapes),
        out_shape=[jax.ShapeDtypeStruct(shape + (LATS,), jnp.bfloat16) for shape in shapes],
        scratch_shapes=[
            pltpu.VMEM(features.shape, jnp.bfloat16),
            pltpu.VMEM(neighbours.shape, jnp.int32),
            pltpu.VMEM((TAP_ROWS, slot_count), jnp.bfloat16),
            pltpu.VMEM((span, rows, LATS), jnp.bfloat16),
            pltpu.SemaphoreType.DMA((groups + 1,)),
            pltpu.SemaphoreType.DMA((groups,)),
            pltpu.SemaphoreType.DMA((2 + targets,)),
        ],
        compiler_params=pltpu.CompilerParams(vmem_limit_bytes=16 * 2**20),
    )(place, features, neighbours)


def over(low, high, body):
    def step(index, carry):
        body(index)
        return carry

    lax.fori_loop(low, jnp.maximum(low, high), step, 0)


def extended(begin, size, live, packed, prev, after, put):
    end = begin + size
    over(begin, jnp.minimum(end, 0), lambda e: put(e - begin, prev, e + DEG))
    over(jnp.maximum(begin, 0), jnp.minimum(end, live), lambda e: put(e - begin, packed, e))
    over(jnp.maximum(begin, live), end, lambda e: put(e - begin, after, jnp.minimum(e - live, DEG - 1)))


def rim_kernel(width, parts, place, packed, prev, after, *rims):
    live, begin = place[0], place[1]

    def copy(offset):
        def put(i, source, column):
            for (low, high), out in zip(parts, rims):
                out[offset + i] = source[column, low:high]

        return put

    extended(begin - DEG, DEG, live, packed, prev, after, copy(0))
    extended(begin + jnp.clip(live - begin, 0, width), DEG, live, packed, prev, after, copy(DEG))


def rims_of(place, packed, prev, after, width, parts):
    shapes = [(2 * DEG, high - low, LATS) for low, high in parts]
    return pl.pallas_call(
        functools.partial(rim_kernel, width, parts),
        in_specs=[SMEM, VMEM, VMEM, VMEM],
        out_specs=[VMEM] * len(shapes),
        out_shape=[jax.ShapeDtypeStruct(shape, jnp.bfloat16) for shape in shapes],
        compiler_params=pltpu.CompilerParams(vmem_limit_bytes=16 * 2**20),
    )(place, packed, prev, after)


def divisor(count, limit):
    return max(d for d in range(1, count + 1) if count % d == 0 and d <= max(limit, 1))


def coefficients(masks, column, value):
    tap = value.astype(jnp.float32)[0:TAPS] * -0.25
    masks[column, 0:8] = jnp.concatenate([pltpu.roll(tap[:, :HALF], HALF - 1, 1), tap[:, HALF:]], axis=1)
    masks[column, 8:16] = tap
    masks[column, 16:24] = jnp.concatenate([tap[:, :HALF], pltpu.roll(tap[:, HALF:], 1, 1)], axis=1)
    own = -2.0 - jnp.sum(tap, axis=0, keepdims=True)
    masks[column, 24:32] = jnp.broadcast_to(own, (8, LATS))


def mask_row(entry):
    index, row = entry // 3, entry % 3
    if entry == 4:
        return 24
    return 8 * row + (entry if entry < 4 else entry - 1)


def chunk_kernel(width, channels, low, last, place, *refs):
    native = low is None
    live, begin, source_channel = place[0], place[1], place[2]
    window = width + 2 * DEG
    refs = list(refs)

    def take(count):
        taken = refs[:count]
        del refs[:count]
        return taken

    if native:
        packed, prev, after, weight, bias, out, masks = take(7)
    else:
        inside, rims, masks, weight, acc, out = take(6)
    *fields, terms, total, held, weight_in, turned, out_sems, sems, column_sems = take(11)
    result = refs[0] if last else total

    rows = pl.ds(pl.multiple_of(source_channel + (0 if native else low), 16), channels)
    weight_copy = pltpu.make_async_copy(weight.at[:, rows], weight_in, sems.at[0])
    if native:

        def fetch(i, source, column):
            pltpu.make_async_copy(source.at[column], held.at[i], column_sems.at[i]).start()

        extended(begin - DEG, window, live, packed, prev, after, fetch)
        weight_copy.start()
    else:
        inside_copy = pltpu.make_async_copy(inside.at[:, pl.ds(low, channels)], held, sems.at[1])
        inside_copy.start()
        weight_copy.start()
        fetch_acc = pltpu.make_async_copy(acc, total, sems.at[2])
        fetch_acc.start()

    def at(column):
        return jnp.clip(column - (DEG - 1), 0, width + 1)

    def load(column, value):
        fields[0][column] = value.astype(jnp.float32)
        terms[at(column), 0:channels] = value

    if native:
        for column in range(window):
            pltpu.make_async_copy(packed.at[0], held.at[column], column_sems.at[column]).wait()
        for column in range(window):
            load(column, held[column, 0:channels])
            coefficients(masks, column, held[column, channels:])
    else:
        for column in range(DEG):
            load(column, rims[column])
        inside_copy.wait()
        for column in range(width):
            load(DEG + column, held[column])
        start = DEG + jnp.clip(live - begin, 0, width)
        for column in range(DEG):
            load(start + column, rims[DEG + column])

    def stencil(level, column):
        newer, older, upcoming = fields[(level - 1) % 3], fields[(level - 2) % 3], fields[level % 3]
        mask = []
        for entry in range(9):
            row = mask_row(entry)
            mask.append(jnp.broadcast_to(masks[column, row : row + 1], (8, LATS)))

        def combine(at, side, values, source):
            lanes = slice(side * HALF, (side + 1) * HALF)
            other = slice(source * HALF, (source + 1) * HALF)
            return (
                mask[at][:, lanes] * values[0][:, other]
                + mask[3 + at][:, lanes] * values[1][:, other]
                + mask[6 + at][:, lanes] * values[2][:, other]
            )

        for base in range(0, channels, 16):
            halves = []
            for row in (base, base + 8):
                rows = slice(row, row + 8)
                values = [newer[column - 1, rows], newer[column, rows], newer[column + 1, rows]]
                even = (
                    combine(1, 0, values, 0) + combine(2, 0, values, 1) + pltpu.roll(combine(0, 0, values, 1), 1, 1)
                )
                odd = (
                    combine(1, 1, values, 1)
                    + combine(0, 1, values, 0)
                    + pltpu.roll(combine(2, 1, values, 0), HALF - 1, 1)
                )
                value = jnp.concatenate([even, odd], axis=1)
                if level == 1:
                    value = 0.5 * value
                else:
                    value = value - older[column, rows]
                if level < DEG:
                    upcoming[column, rows] = value
                halves.append(value)
            place_in = level * channels + base
            terms[at(column), place_in : place_in + 16] = jnp.concatenate(halves, axis=0).astype(jnp.bfloat16)

    def together(level):
        return divisor(window - 2 * level, 52 * 8 // channels)

    for level in range(1, DEG):
        group = together(level)

        def step(index):
            for member in range(group):
                stencil(level, level + index * group + member)

        over(0, (window - 2 * level) // group, step)

    weight_copy.wait()
    turned[...] = weight_in[...].reshape((DEG + 1) * channels, -1).T
    if not native:
        fetch_acc.wait()
    sort = sorting() if last else None

    def send(column):
        return pltpu.make_async_copy(result.at[column], out.at[column], out_sems.at[column])

    def mix(column):
        product = jnp.dot(turned[...], terms[1 + column], preferred_element_type=jnp.float32)
        product = product + (bias[...] if native else total[column])
        if last:
            alive = (begin + column < live).astype(jnp.float32)
            product = (product * alive).astype(jnp.bfloat16)
            product = lax.dot_general(
                sort, product, (((1,), (1,)), ((), ())), preferred_element_type=jnp.float32
            ).astype(jnp.bfloat16)
        result[column] = product

    group = together(DEG)

    def finish(index):
        for member in range(group):
            mix(index * group + member)
        for member in range(group):
            send(index * group + member).start()

    def outermost(index):
        for member in range(group):
            stencil(DEG, DEG + index * group + member)

    outermost(0)

    def both(index):
        outermost(index)
        finish(index - 1)

    over(1, width // group, both)
    finish(width // group - 1)
    for column in range(width):
        send(column).wait()


def chunk_step(place, width, channels, low, last, operands, outs):
    native = low is None
    window = width + 2 * DEG
    out_shape = [jax.ShapeDtypeStruct((width, LATS, outs), jnp.bfloat16 if last else jnp.float32)]
    out_specs = [ANY]
    if native:
        specs = [SMEM, ANY, ANY, ANY, ANY, VMEM]
        out_shape.append(jax.ShapeDtypeStruct((window, 32, LATS), jnp.float32))
        out_specs.append(VMEM)
        held = (window, channels + TAP_ROWS, LATS)
    else:
        specs = [SMEM, ANY, VMEM, VMEM, ANY, ANY]
        held = (width, channels, LATS)
    scratch = [pltpu.VMEM((window, channels, LATS), jnp.float32)] * 3
    scratch.append(pltpu.VMEM((width + 2, (DEG + 1) * channels, LATS), jnp.bfloat16))
    scratch.append(pltpu.VMEM((width, outs, LATS), jnp.float32))
    scratch.append(pltpu.VMEM(held, jnp.bfloat16))
    scratch.append(pltpu.VMEM((DEG + 1, channels, outs), jnp.bfloat16))
    scratch.append(pltpu.VMEM((outs, (DEG + 1) * channels), jnp.bfloat16))
    scratch.append(pltpu.SemaphoreType.DMA((width,)))
    scratch.append(pltpu.SemaphoreType.DMA((3,)))
    scratch.append(pltpu.SemaphoreType.DMA((window,)))
    if last:
        scratch.append(pltpu.VMEM((width, LATS, outs), jnp.bfloat16))
    return pl.pallas_call(
        functools.partial(chunk_kernel, width, channels, low, last),
        out_shape=out_shape,
        in_specs=specs,
        out_specs=out_specs,
        scratch_shapes=scratch,
        compiler_params=pltpu.CompilerParams(vmem_limit_bytes=(40 if native else 28) * 2**20),
    )(place, *operands)


def splits(native):
    if native % 64:
        return [(0, native)]
    return [(0, native // 2), (native // 2, 3 * native // 4), (3 * native // 4, native)]


def shards(features, neighbours, live_cols, cheb_weight, out_bias):
    native, slot_count = features.shape
    outs = cheb_weight.shape[2]
    count = lax.axis_size("chan")
    me = lax.axis_index("chan")
    width = slot_count // LATS // count
    live = live_cols[0]
    parts = splits(native)
    targets = [lax.rem(me + distance, count) * width for distance in range(1, count)]
    packed, last_cols, first_cols, *early = pack(
        features, neighbours, jnp.stack([live] + targets), width, count - 1
    )
    insides = [shifted(early[distance - 1], "chan", distance) for distance in range(1, count)]
    prev = shifted(last_cols, ("pix", "sub"), 1)
    after = shifted(first_cols, ("pix", "sub"), -1)
    blocks = []
    for distance in range(1, count):
        place = jnp.stack([live, targets[distance - 1]])
        rims = rims_of(place, packed, prev, after, width, parts)
        for part, value in zip(parts, rims):
            blocks.append((distance, part, shifted(value, "chan", distance)))

    def place_of(distance):
        source = lax.rem(me - distance + count, count)
        return jnp.stack([live, me * width, source * native])

    bias = jnp.broadcast_to(out_bias[:, None], (outs, LATS))
    acc, masks = chunk_step(
        place_of(0), width, native, None, False, [packed, prev, after, cheb_weight, bias], outs
    )
    for index, (distance, (low, high), rims) in enumerate(blocks):
        operands = [insides[distance - 1], rims, masks, cheb_weight, acc]
        last = index == len(blocks) - 1
        (acc,) = chunk_step(place_of(distance), width, high - low, low, last, operands, outs)
    return acc.reshape(1, width * LATS, acc.shape[2])


def solution(mesh):
    in_specs = (
        P("chan", ("grp", "pix", "sub")),
        P(None, ("grp", "pix", "sub")),
        P(("grp", "pix", "sub")),
        P(),
        P(),
    )
    out_specs = P(("grp", "pix", "sub"), "chan", None)
    return jax.shard_map(shards, mesh=mesh, in_specs=in_specs, out_specs=out_specs, check_vma=False)
```

time: 373 us -> 71.4 us (0.19)
  the two profiles are of different devices: /device:TPU:0 before, /device:TPU:1 now
where the time goes in v2:
time: 71.4 us; the launch traced here: 71.2 us
  Pallas kernels  46 us (64%)
  waiting for transfers between devices  12.7 us (18%)
  starting transfers between devices  5.76 us (8%)
  local copies, waits for them, and re-layouts  5.73 us (8%)
  between operations  0.83 us (1%)
    pallas_call x4, Pallas kernels, chunk_step(): pl.pallas_call(functools.partial(chunk_kernel, width, channels, low, last...  40.8 us
    ppermute x6, waiting for transfers between devices, shifted(): return lax.ppermute(value, axis, pairs)  12.7 us
    ppermute x6, starting transfers between devices, shifted(): return lax.ppermute(value, axis, pairs)  5.76 us
    unnamed x12, local copies, waits for them, and re-layouts  5.63 us
    pallas_call x1, Pallas kernels, pack(): pl.pallas_call(functools.partial(pack_kernel, span, width, targets, group...  3.63 us
    pallas_call x1, Pallas kernels, rims_of(): pl.pallas_call(functools.partial(rim_kernel, width, parts), in_specs=[SME...  1.58 us
  transfers between devices with their start and end apart: 6, of which 2 were waited for; matrix products, arithmetic and copies ran while one was open for 0% of the time, Pallas kernels for 51%

profile of v2, /device:TPU:1, one launch (start us, length us, event | category | flops | bytes accessed | tf_op | source)
XLA Modules:
  0.0 71.2 jit_solution(13109572506777658712)
XLA Ops:
  0.0 0.0 copy-start
  0.7 0.1 pad_add_fusion.2.place
  0.8 0.0 copy-start.3
  0.8 1.6 %copy-done.3 = bf16[128,8192]{1,0:T(8,128)(2,1)S(1)} copy-done((bf16[128,8192]{1,0:T(8,128)(2,1)S(1)}, bf16[128,8192]{1,0:T(8,128)(2,1)}, u32[]{:S(2)}) %copy-start.3) | copy-done | bytes 2097176
  2.4 0.0 copy-start.4
  2.4 0.9 %copy-done.4 = s32[8,8192]{1,0:T(8,128)S(1)} copy-done((s32[8,8192]{1,0:T(8,128)S(1)}, s32[8,8192]{1,0:T(8,128)}, u32[]{:S(2)}) %copy-start.4) | copy-done | bytes 262168
  3.4 0.0 copy-start.5
  3.4 3.6 %shard_map.55 = (bf16[32,144,256]{2,1,0:T(8,128)(2,1)S(1)}, bf16[6,144,256]{2,1,0:T(8,128)(2,1)S(1)}, bf16[6,144,256]{2,1,0:T(8,128)(2,1)S(1)}, bf16[16,128,256]{2,1,0:T(8,128)(2,1)}) custom-call(s32[2]{0:T(128)S(1)} %pad_add_fusion.2.place, bf16[128,8192]{1,0:T(8,128)(2,1)S(1)} %copy-done.3, s32[8,8192]{1,0:T(8,128)S(1)} %copy-done.4), custom_call_target="tpu_custom_call" | custom-call | tf_op jit(solution)/shard_map/pallas_call | solution.py:80
  7.0 2.1 %collective-permute-start = (bf16[16,128,256]{2,1,0:T(8,128)(2,1)}, bf16[16,128,256]{2,1,0:T(8,128)(2,1)S(1)}, u32[]{:S(2)}, u32[]{:S(2)}) collective-permute-start(bf16[16,128,256]{2,1,0:T(8,128)(2,1)} %get-tuple-element.14), channel_id=1, source_target_pairs={{0,2},{2,0},{1,3},{3,1},{4,6},{6,4},{5,7},{7,5},{8,10},{10,8},{9,1... | collective-permute-start | bytes 3145736 | tf_op jit(solution)/shard_map/ppermute | solution.py:20
  9.1 2.1 %collective-permute-start.1 = (bf16[6,144,256]{2,1,0:T(8,128)(2,1)S(1)}, bf16[6,144,256]{2,1,0:T(8,128)(2,1)S(1)}, u32[]{:S(2)}, u32[]{:S(2)}) collective-permute-start(bf16[6,144,256]{2,1,0:T(8,128)(2,1)S(1)} %get-tuple-element.16), channel_id=1, source_target_pairs={{0,1},{1,4},{4,5},{5,8},{8,9},{9,12},{12,13},{13,0},{2,3},{3,6},{6... | collective-permute-start | bytes 1327112 | tf_op jit(solution)/shard_map/ppermute | solution.py:20
  11.2 0.0 collective-permute-start.2
  11.2 7.4 %collective-permute-done.1.prev.refs_1_ = bf16[6,144,256]{2,1,0:T(8,128)(2,1)S(1)} collective-permute-done((bf16[6,144,256]{2,1,0:T(8,128)(2,1)S(1)}, bf16[6,144,256]{2,1,0:T(8,128)(2,1)S(1)}, u32[]{:S(2)}, u32[]{:S(2)}) %collective-permute-start.1) | collective-permute-done | bytes 442400 | tf_op jit(solution)/shard_map/ppermute | solution.py:20
  18.6 5.3 %collective-permute-done.2.after.refs_2_ = bf16[6,144,256]{2,1,0:T(8,128)(2,1)S(1)} collective-permute-done((bf16[6,144,256]{2,1,0:T(8,128)(2,1)S(1)}, bf16[6,144,256]{2,1,0:T(8,128)(2,1)S(1)}, u32[]{:S(2)}, u32[]{:S(2)}) %collective-permute-start.2) | collective-permute-done | bytes 442400 | tf_op jit(solution)/shard_map/ppermute | solution.py:20
  23.9 1.6 %shard_map.56 = (bf16[12,64,256]{2,1,0:T(8,128)(2,1)}, bf16[12,32,256]{2,1,0:T(8,128)(2,1)}, bf16[12,32,256]{2,1,0:T(8,128)(2,1)}) custom-call(s32[2]{0:T(128)S(1)} %pad_add_fusion.2.place, bf16[32,144,256]{2,1,0:T(8,128)(2,1)S(1)} %get-tuple-element.15.packed.refs_0_, bf16[6,144,256]{2,1,0:T(8,128)(2,1)S(1)} %collective-permute-done.1.prev.refs_1_, ...), custom_call_target="tpu_custom_call" | custom-call | tf_op jit(solution)/shard_map/pallas_call | solution.py:129
  25.5 0.0 copy-start.1
  25.5 1.4 %copy-done.1 = bf16[32,144,256]{2,1,0:T(8,128)(2,1)} copy-done((bf16[32,144,256]{2,1,0:T(8,128)(2,1)}, bf16[32,144,256]{2,1,0:T(8,128)(2,1)S(1)}, u32[]{:S(2)}) %copy-start.1) | copy-done | bytes 2359320
  26.9 0.0 collective-permute-start.5
  26.9 1.5 %collective-permute-start.4 = (bf16[12,32,256]{2,1,0:T(8,128)(2,1)}, bf16[12,32,256]{2,1,0:T(8,128)(2,1)}, u32[]{:S(2)}, u32[]{:S(2)}) collective-permute-start(bf16[12,32,256]{2,1,0:T(8,128)(2,1)} %get-tuple-element.20), channel_id=1, source_target_pairs={{0,2},{2,0},{1,3},{3,1},{4,6},{6,4},{5,7},{7,5},{8,10},{10,8},{9,1... | collective-permute-start | bytes 589832 | tf_op jit(solution)/shard_map/ppermute | solution.py:20
  28.4 0.0 collective-permute-start.3
  28.5 0.1 pad_add_fusion
  28.5 0.0 copy-done.5
  28.5 0.1 broadcast_in_dim.2.refs_4_
  28.6 0.0 copy-done
  28.6 0.0 copy-start.2
  28.7 1.7 %copy-done.2 = bf16[32,144,256]{2,1,0:T(8,128)(2,1)S(1)} copy-done((bf16[32,144,256]{2,1,0:T(8,128)(2,1)S(1)}, bf16[32,144,256]{2,1,0:T(8,128)(2,1)}, u32[]{:S(2)}) %copy-start.2) | copy-done | bytes 2359320
  30.3 19.1 %shard_map.57 = (f32[16,256,256]{2,1,0:T(8,128)S(1)}, f32[28,32,256]{2,1,0:T(8,128)S(1)}) custom-call(s32[3]{0:T(128)S(1)} %get-tuple-element.24.place, bf16[32,144,256]{2,1,0:T(8,128)(2,1)S(1)} %copy-done.2, bf16[6,144,256]{2,1,0:T(8,128)(2,1)S(1)} %collective-permute-done.1.prev.refs_1_, bf16[6,144,256]{2,1,0:T(8,128)(2,1)S(1)} %collective-permute-done.2.after.refs_2_, ...), custom_call_target="tpu_custom_call" | custom-call | tf_op jit(solution)/shard_map/pallas_call | solution.py:335
  49.4 0.0 collective-permute-done.5.refs_1_
  49.5 0.0 collective-permute-done.refs_0_
  49.5 9.8 %shard_map.58.refs_4_ = f32[16,256,256]{2,1,0:T(8,128)S(1)} custom-call(s32[3]{0:T(128)S(1)} %get-tuple-element.23.place, bf16[16,128,256]{2,1,0:T(8,128)(2,1)S(1)} %collective-permute-done.refs_0_, bf16[12,64,256]{2,1,0:T(8,128)(2,1)S(1)} %collective-permute-done.5.refs_1_, f32[28,32,256]{2,1,0:T(8,128)S(1)} %get-tuple-element.19.refs_2_, ...), custom_call_target="tpu_custom_call" | custom-call | tf_op jit(solution)/shard_map/pallas_call | solution.py:335
  59.2 0.0 collective-permute-done.4.refs_1_
  59.3 5.6 %shard_map.59.refs_4_ = f32[16,256,256]{2,1,0:T(8,128)S(1)} custom-call(s32[3]{0:T(128)S(1)} %get-tuple-element.23.place, bf16[16,128,256]{2,1,0:T(8,128)(2,1)S(1)} %collective-permute-done.refs_0_, bf16[12,32,256]{2,1,0:T(8,128)(2,1)} %collective-permute-done.4.refs_1_, f32[28,32,256]{2,1,0:T(8,128)S(1)} %get-tuple-element.19.refs_2_, ...), custom_call_target="tpu_custom_call" | custom-call | tf_op jit(solution)/shard_map/pallas_call | solution.py:335
  64.8 0.0 collective-permute-done.3.refs_1_
  64.8 6.3 %shard_map.60 = bf16[16,256,256]{2,1,0:T(8,128)(2,1)} custom-call(s32[3]{0:T(128)S(1)} %get-tuple-element.23.place, bf16[16,128,256]{2,1,0:T(8,128)(2,1)S(1)} %collective-permute-done.refs_0_, bf16[12,32,256]{2,1,0:T(8,128)(2,1)S(1)} %collective-permute-done.3.refs_1_, f32[28,32,256]{2,1,0:T(8,128)S(1)} %get-tuple-element.19.refs_2_, ...), custom_call_target="tpu_custom_call" | custom-call | tf_op jit(solution)/shard_map/pallas_call | solution.py:335
Async XLA Ops:
  0.0 28.6 %copy-start = (bf16[7,256,256]{2,1,0:T(8,128)(2,1)S(1)}, bf16[7,256,256]{2,1,0:T(8,128)(2,1)}, u32[]{:S(2)}) copy-start(bf16[7,256,256]{2,1,0:T(8,128)(2,1)} %refs_3_.7) | copy-start | bytes 2752516
  0.8 1.6 %copy-start.3 = (bf16[128,8192]{1,0:T(8,128)(2,1)S(1)}, bf16[128,8192]{1,0:T(8,128)(2,1)}, u32[]{:S(2)}) copy-start(bf16[128,8192]{1,0:T(8,128)(2,1)} %features.1) | copy-start | bytes 6291460
  2.4 0.9 %copy-start.4 = (s32[8,8192]{1,0:T(8,128)S(1)}, s32[8,8192]{1,0:T(8,128)}, u32[]{:S(2)}) copy-start(s32[8,8192]{1,0:T(8,128)} %neighbours.1) | copy-start | bytes 786436
  3.4 25.2 %copy-start.5 = (f32[256]{0:T(256)S(1)}, f32[256]{0:T(256)}, u32[]{:S(2)}) copy-start(f32[256]{0:T(256)} %param.9) | copy-start | bytes 3076
  7.0 42.5 %collective-permute-start = (bf16[16,128,256]{2,1,0:T(8,128)(2,1)}, bf16[16,128,256]{2,1,0:T(8,128)(2,1)S(1)}, u32[]{:S(2)}, u32[]{:S(2)}) collective-permute-start(bf16[16,128,256]{2,1,0:T(8,128)(2,1)} %get-tuple-element.14), channel_id=1, source_target_pairs={{0,2},{2,0},{1,3},{3,1},{4,6},{6,4},{5,7},{7,5},{8,10},{10,8},{9,1... | collective-permute-start | bytes 3145736 | tf_op jit(solution)/shard_map/ppermute | solution.py:20
  9.1 9.5 %collective-permute-start.1 = (bf16[6,144,256]{2,1,0:T(8,128)(2,1)S(1)}, bf16[6,144,256]{2,1,0:T(8,128)(2,1)S(1)}, u32[]{:S(2)}, u32[]{:S(2)}) collective-permute-start(bf16[6,144,256]{2,1,0:T(8,128)(2,1)S(1)} %get-tuple-element.16), channel_id=1, source_target_pairs={{0,1},{1,4},{4,5},{5,8},{8,9},{9,12},{12,13},{13,0},{2,3},{3,6},{6... | collective-permute-start | bytes 1327112 | tf_op jit(solution)/shard_map/ppermute | solution.py:20
  11.2 12.7 %collective-permute-start.2 = (bf16[6,144,256]{2,1,0:T(8,128)(2,1)S(1)}, bf16[6,144,256]{2,1,0:T(8,128)(2,1)S(1)}, u32[]{:S(2)}, u32[]{:S(2)}) collective-permute-start(bf16[6,144,256]{2,1,0:T(8,128)(2,1)S(1)} %get-tuple-element.17), channel_id=1, source_target_pairs={{0,13},{1,0},{4,1},{5,4},{8,5},{9,8},{12,9},{13,12},{2,15},{3,2},{... | collective-permute-start | bytes 1327112 | tf_op jit(solution)/shard_map/ppermute | solution.py:20
  25.5 1.4 %copy-start.1 = (bf16[32,144,256]{2,1,0:T(8,128)(2,1)}, bf16[32,144,256]{2,1,0:T(8,128)(2,1)S(1)}, u32[]{:S(2)}) copy-start(bf16[32,144,256]{2,1,0:T(8,128)(2,1)S(1)} %get-tuple-element.15.packed.refs_0_) | copy-start | bytes 7077892
  26.9 22.5 %collective-permute-start.5 = (bf16[12,64,256]{2,1,0:T(8,128)(2,1)}, bf16[12,64,256]{2,1,0:T(8,128)(2,1)S(1)}, u32[]{:S(2)}, u32[]{:S(2)}) collective-permute-start(bf16[12,64,256]{2,1,0:T(8,128)(2,1)} %get-tuple-element.21), channel_id=1, source_target_pairs={{0,2},{2,0},{1,3},{3,1},{4,6},{6,4},{5,7},{7,5},{8,10},{10,8},{9,1... | collective-permute-start | bytes 1179656 | tf_op jit(solution)/shard_map/ppermute | solution.py:20
  26.9 32.3 %collective-permute-start.4 = (bf16[12,32,256]{2,1,0:T(8,128)(2,1)}, bf16[12,32,256]{2,1,0:T(8,128)(2,1)}, u32[]{:S(2)}, u32[]{:S(2)}) collective-permute-start(bf16[12,32,256]{2,1,0:T(8,128)(2,1)} %get-tuple-element.20), channel_id=1, source_target_pairs={{0,2},{2,0},{1,3},{3,1},{4,6},{6,4},{5,7},{7,5},{8,10},{10,8},{9,1... | collective-permute-start | bytes 589832 | tf_op jit(solution)/shard_map/ppermute | solution.py:20
  28.4 36.4 %collective-permute-start.3 = (bf16[12,32,256]{2,1,0:T(8,128)(2,1)}, bf16[12,32,256]{2,1,0:T(8,128)(2,1)S(1)}, u32[]{:S(2)}, u32[]{:S(2)}) collective-permute-start(bf16[12,32,256]{2,1,0:T(8,128)(2,1)} %get-tuple-element.18), channel_id=1, source_target_pairs={{0,2},{2,0},{1,3},{3,1},{4,6},{6,4},{5,7},{7,5},{8,10},{10,8},{9,1... | collective-permute-start | bytes 589832 | tf_op jit(solution)/shard_map/ppermute | solution.py:20
  28.6 1.7 %copy-start.2 = (bf16[32,144,256]{2,1,0:T(8,128)(2,1)S(1)}, bf16[32,144,256]{2,1,0:T(8,128)(2,1)}, u32[]{:S(2)}) copy-start(bf16[32,144,256]{2,1,0:T(8,128)(2,1)} %copy-done.1) | copy-start | bytes 7077892

commit v3 on v2

--- a/solution.py
+++ b/solution.py
@@ -253,7 +253,7 @@
             terms[at(column), place_in : place_in + 16] = jnp.concatenate(halves, axis=0).astype(jnp.bfloat16)
 
     def together(level):
-        return divisor(window - 2 * level, 52 * 8 // channels)
+        return divisor(window - 2 * level, max(4, 416 // channels))
 
     for level in range(1, DEG):
         group = together(level)
@@ -338,7 +338,7 @@
         in_specs=specs,
         out_specs=out_specs,
         scratch_shapes=scratch,
-        compiler_params=pltpu.CompilerParams(vmem_limit_bytes=(40 if native else 28) * 2**20),
+        compiler_params=pltpu.CompilerParams(vmem_limit_bytes=40 * 2**20),
     )(place, *operands)
 
 

time: 71.4 us -> 70.7 us (level)
    pallas_call x4, Pallas kernels: 40.8 us -> 40.1 us  [chunk_step(): pl.pallas_call(functools.partial(chunk_kernel, width, channels, low, last...]
  transfers between devices with their start and end apart: 6 -> 6, of which waited for: 2 -> 2; matrix products, arithmetic and copies ran while one was open for 0% -> 0% of each run, Pallas kernels for 51% -> 50%
where the time goes in v3:
time: 70.7 us; the launch traced here: 70.4 us
  Pallas kernels  45.3 us (64%)
  waiting for transfers between devices  12.7 us (18%)
  starting transfers between devices  5.76 us (8%)
  local copies, waits for them, and re-layouts  5.73 us (8%)
  between operations  0.83 us (1%)
    pallas_call x4, Pallas kernels, chunk_step(): pl.pallas_call(functools.partial(chunk_kernel, width, channels, low, last...  40.1 us
    ppermute x6, waiting for transfers between devices, shifted(): return lax.ppermute(value, axis, pairs)  12.7 us
    ppermute x6, starting transfers between devices, shifted(): return lax.ppermute(value, axis, pairs)  5.76 us
    unnamed x12, local copies, waits for them, and re-layouts  5.63 us
    pallas_call x1, Pallas kernels, pack(): pl.pallas_call(functools.partial(pack_kernel, span, width, targets, group...  3.63 us
    pallas_call x1, Pallas kernels, rims_of(): pl.pallas_call(functools.partial(rim_kernel, width, parts), in_specs=[SME...  1.58 us
  transfers between devices with their start and end apart: 6, of which 2 were waited for; matrix products, arithmetic and copies ran while one was open for 0% of the time, Pallas kernels for 50%

profile of v3, /device:TPU:1, one launch (start us, length us, event | category | flops | bytes accessed | tf_op | source)
XLA Modules:
  0.0 70.4 jit_solution(11847044808330332111)
XLA Ops:
  0.0 0.0 copy-start
  0.7 0.1 pad_add_fusion.2.place
  0.8 0.0 copy-start.3
  0.8 1.6 %copy-done.3 = bf16[128,8192]{1,0:T(8,128)(2,1)S(1)} copy-done((bf16[128,8192]{1,0:T(8,128)(2,1)S(1)}, bf16[128,8192]{1,0:T(8,128)(2,1)}, u32[]{:S(2)}) %copy-start.3) | copy-done | bytes 2097176
  2.4 0.0 copy-start.4
  2.4 0.9 %copy-done.4 = s32[8,8192]{1,0:T(8,128)S(1)} copy-done((s32[8,8192]{1,0:T(8,128)S(1)}, s32[8,8192]{1,0:T(8,128)}, u32[]{:S(2)}) %copy-start.4) | copy-done | bytes 262168
  3.4 0.0 copy-start.5
  3.4 3.6 %shard_map.55 = (bf16[32,144,256]{2,1,0:T(8,128)(2,1)S(1)}, bf16[6,144,256]{2,1,0:T(8,128)(2,1)S(1)}, bf16[6,144,256]{2,1,0:T(8,128)(2,1)S(1)}, bf16[16,128,256]{2,1,0:T(8,128)(2,1)}) custom-call(s32[2]{0:T(128)S(1)} %pad_add_fusion.2.place, bf16[128,8192]{1,0:T(8,128)(2,1)S(1)} %copy-done.3, s32[8,8192]{1,0:T(8,128)S(1)} %copy-done.4), custom_call_target="tpu_custom_call" | custom-call | tf_op jit(solution)/shard_map/pallas_call | solution.py:80
  7.0 2.1 %collective-permute-start = (bf16[16,128,256]{2,1,0:T(8,128)(2,1)}, bf16[16,128,256]{2,1,0:T(8,128)(2,1)S(1)}, u32[]{:S(2)}, u32[]{:S(2)}) collective-permute-start(bf16[16,128,256]{2,1,0:T(8,128)(2,1)} %get-tuple-element.14), channel_id=1, source_target_pairs={{0,2},{2,0},{1,3},{3,1},{4,6},{6,4},{5,7},{7,5},{8,10},{10,8},{9,1... | collective-permute-start | bytes 3145736 | tf_op jit(solution)/shard_map/ppermute | solution.py:20
  9.1 2.1 %collective-permute-start.1 = (bf16[6,144,256]{2,1,0:T(8,128)(2,1)S(1)}, bf16[6,144,256]{2,1,0:T(8,128)(2,1)S(1)}, u32[]{:S(2)}, u32[]{:S(2)}) collective-permute-start(bf16[6,144,256]{2,1,0:T(8,128)(2,1)S(1)} %get-tuple-element.16), channel_id=1, source_target_pairs={{0,1},{1,4},{4,5},{5,8},{8,9},{9,12},{12,13},{13,0},{2,3},{3,6},{6... | collective-permute-start | bytes 1327112 | tf_op jit(solution)/shard_map/ppermute | solution.py:20
  11.2 0.0 collective-permute-start.2
  11.2 7.4 %collective-permute-done.1.prev.refs_1_ = bf16[6,144,256]{2,1,0:T(8,128)(2,1)S(1)} collective-permute-done((bf16[6,144,256]{2,1,0:T(8,128)(2,1)S(1)}, bf16[6,144,256]{2,1,0:T(8,128)(2,1)S(1)}, u32[]{:S(2)}, u32[]{:S(2)}) %collective-permute-start.1) | collective-permute-done | bytes 442400 | tf_op jit(solution)/shard_map/ppermute | solution.py:20
  18.6 5.3 %collective-permute-done.2.after.refs_2_ = bf16[6,144,256]{2,1,0:T(8,128)(2,1)S(1)} collective-permute-done((bf16[6,144,256]{2,1,0:T(8,128)(2,1)S(1)}, bf16[6,144,256]{2,1,0:T(8,128)(2,1)S(1)}, u32[]{:S(2)}, u32[]{:S(2)}) %collective-permute-start.2) | collective-permute-done | bytes 442400 | tf_op jit(solution)/shard_map/ppermute | solution.py:20
  23.9 1.6 %shard_map.56 = (bf16[12,64,256]{2,1,0:T(8,128)(2,1)}, bf16[12,32,256]{2,1,0:T(8,128)(2,1)}, bf16[12,32,256]{2,1,0:T(8,128)(2,1)}) custom-call(s32[2]{0:T(128)S(1)} %pad_add_fusion.2.place, bf16[32,144,256]{2,1,0:T(8,128)(2,1)S(1)} %get-tuple-element.15.packed.refs_0_, bf16[6,144,256]{2,1,0:T(8,128)(2,1)S(1)} %collective-permute-done.1.prev.refs_1_, ...), custom_call_target="tpu_custom_call" | custom-call | tf_op jit(solution)/shard_map/pallas_call | solution.py:129
  25.5 0.0 copy-start.1
  25.5 1.4 %copy-done.1 = bf16[32,144,256]{2,1,0:T(8,128)(2,1)} copy-done((bf16[32,144,256]{2,1,0:T(8,128)(2,1)}, bf16[32,144,256]{2,1,0:T(8,128)(2,1)S(1)}, u32[]{:S(2)}) %copy-start.1) | copy-done | bytes 2359320
  26.9 0.0 collective-permute-start.5
  26.9 1.5 %collective-permute-start.4 = (bf16[12,32,256]{2,1,0:T(8,128)(2,1)}, bf16[12,32,256]{2,1,0:T(8,128)(2,1)}, u32[]{:S(2)}, u32[]{:S(2)}) collective-permute-start(bf16[12,32,256]{2,1,0:T(8,128)(2,1)} %get-tuple-element.20), channel_id=1, source_target_pairs={{0,2},{2,0},{1,3},{3,1},{4,6},{6,4},{5,7},{7,5},{8,10},{10,8},{9,1... | collective-permute-start | bytes 589832 | tf_op jit(solution)/shard_map/ppermute | solution.py:20
  28.4 0.0 collective-permute-start.3
  28.5 0.1 pad_add_fusion
  28.5 0.0 copy-done.5
  28.5 0.1 broadcast_in_dim.2.refs_4_
  28.6 0.0 copy-done
  28.6 0.0 copy-start.2
  28.7 1.7 %copy-done.2 = bf16[32,144,256]{2,1,0:T(8,128)(2,1)S(1)} copy-done((bf16[32,144,256]{2,1,0:T(8,128)(2,1)S(1)}, bf16[32,144,256]{2,1,0:T(8,128)(2,1)}, u32[]{:S(2)}) %copy-start.2) | copy-done | bytes 2359320
  30.3 18.4 %shard_map.57 = (f32[16,256,256]{2,1,0:T(8,128)S(1)}, f32[28,32,256]{2,1,0:T(8,128)S(1)}) custom-call(s32[3]{0:T(128)S(1)} %get-tuple-element.24.place, bf16[32,144,256]{2,1,0:T(8,128)(2,1)S(1)} %copy-done.2, bf16[6,144,256]{2,1,0:T(8,128)(2,1)S(1)} %collective-permute-done.1.prev.refs_1_, bf16[6,144,256]{2,1,0:T(8,128)(2,1)S(1)} %collective-permute-done.2.after.refs_2_, ...), custom_call_target="tpu_custom_call" | custom-call | tf_op jit(solution)/shard_map/pallas_call | solution.py:335
  48.7 0.0 collective-permute-done.5.refs_1_
  48.7 0.0 collective-permute-done.refs_0_
  48.7 9.8 %shard_map.58.refs_4_ = f32[16,256,256]{2,1,0:T(8,128)S(1)} custom-call(s32[3]{0:T(128)S(1)} %get-tuple-element.23.place, bf16[16,128,256]{2,1,0:T(8,128)(2,1)S(1)} %collective-permute-done.refs_0_, bf16[12,64,256]{2,1,0:T(8,128)(2,1)S(1)} %collective-permute-done.5.refs_1_, f32[28,32,256]{2,1,0:T(8,128)S(1)} %get-tuple-element.19.refs_2_, ...), custom_call_target="tpu_custom_call" | custom-call | tf_op jit(solution)/shard_map/pallas_call | solution.py:335
  58.5 0.0 collective-permute-done.4.refs_1_
  58.5 5.6 %shard_map.59.refs_4_ = f32[16,256,256]{2,1,0:T(8,128)S(1)} custom-call(s32[3]{0:T(128)S(1)} %get-tuple-element.23.place, bf16[16,128,256]{2,1,0:T(8,128)(2,1)S(1)} %collective-permute-done.refs_0_, bf16[12,32,256]{2,1,0:T(8,128)(2,1)} %collective-permute-done.4.refs_1_, f32[28,32,256]{2,1,0:T(8,128)S(1)} %get-tuple-element.19.refs_2_, ...), custom_call_target="tpu_custom_call" | custom-call | tf_op jit(solution)/shard_map/pallas_call | solution.py:335
  64.1 0.0 collective-permute-done.3.refs_1_
  64.1 6.3 %shard_map.60 = bf16[16,256,256]{2,1,0:T(8,128)(2,1)} custom-call(s32[3]{0:T(128)S(1)} %get-tuple-element.23.place, bf16[16,128,256]{2,1,0:T(8,128)(2,1)S(1)} %collective-permute-done.refs_0_, bf16[12,32,256]{2,1,0:T(8,128)(2,1)S(1)} %collective-permute-done.3.refs_1_, f32[28,32,256]{2,1,0:T(8,128)S(1)} %get-tuple-element.19.refs_2_, ...), custom_call_target="tpu_custom_call" | custom-call | tf_op jit(solution)/shard_map/pallas_call | solution.py:335
Async XLA Ops:
  0.0 28.6 %copy-start = (bf16[7,256,256]{2,1,0:T(8,128)(2,1)S(1)}, bf16[7,256,256]{2,1,0:T(8,128)(2,1)}, u32[]{:S(2)}) copy-start(bf16[7,256,256]{2,1,0:T(8,128)(2,1)} %refs_3_.7) | copy-start | bytes 2752516
  0.8 1.6 %copy-start.3 = (bf16[128,8192]{1,0:T(8,128)(2,1)S(1)}, bf16[128,8192]{1,0:T(8,128)(2,1)}, u32[]{:S(2)}) copy-start(bf16[128,8192]{1,0:T(8,128)(2,1)} %features.1) | copy-start | bytes 6291460
  2.4 0.9 %copy-start.4 = (s32[8,8192]{1,0:T(8,128)S(1)}, s32[8,8192]{1,0:T(8,128)}, u32[]{:S(2)}) copy-start(s32[8,8192]{1,0:T(8,128)} %neighbours.1) | copy-start | bytes 786436
  3.4 25.2 %copy-start.5 = (f32[256]{0:T(256)S(1)}, f32[256]{0:T(256)}, u32[]{:S(2)}) copy-start(f32[256]{0:T(256)} %param.9) | copy-start | bytes 3076
  7.0 41.7 %collective-permute-start = (bf16[16,128,256]{2,1,0:T(8,128)(2,1)}, bf16[16,128,256]{2,1,0:T(8,128)(2,1)S(1)}, u32[]{:S(2)}, u32[]{:S(2)}) collective-permute-start(bf16[16,128,256]{2,1,0:T(8,128)(2,1)} %get-tuple-element.14), channel_id=1, source_target_pairs={{0,2},{2,0},{1,3},{3,1},{4,6},{6,4},{5,7},{7,5},{8,10},{10,8},{9,1... | collective-permute-start | bytes 3145736 | tf_op jit(solution)/shard_map/ppermute | solution.py:20
  9.1 9.5 %collective-permute-start.1 = (bf16[6,144,256]{2,1,0:T(8,128)(2,1)S(1)}, bf16[6,144,256]{2,1,0:T(8,128)(2,1)S(1)}, u32[]{:S(2)}, u32[]{:S(2)}) collective-permute-start(bf16[6,144,256]{2,1,0:T(8,128)(2,1)S(1)} %get-tuple-element.16), channel_id=1, source_target_pairs={{0,1},{1,4},{4,5},{5,8},{8,9},{9,12},{12,13},{13,0},{2,3},{3,6},{6... | collective-permute-start | bytes 1327112 | tf_op jit(solution)/shard_map/ppermute | solution.py:20
  11.2 12.7 %collective-permute-start.2 = (bf16[6,144,256]{2,1,0:T(8,128)(2,1)S(1)}, bf16[6,144,256]{2,1,0:T(8,128)(2,1)S(1)}, u32[]{:S(2)}, u32[]{:S(2)}) collective-permute-start(bf16[6,144,256]{2,1,0:T(8,128)(2,1)S(1)} %get-tuple-element.17), channel_id=1, source_target_pairs={{0,13},{1,0},{4,1},{5,4},{8,5},{9,8},{12,9},{13,12},{2,15},{3,2},{... | collective-permute-start | bytes 1327112 | tf_op jit(solution)/shard_map/ppermute | solution.py:20
  25.5 1.4 %copy-start.1 = (bf16[32,144,256]{2,1,0:T(8,128)(2,1)}, bf16[32,144,256]{2,1,0:T(8,128)(2,1)S(1)}, u32[]{:S(2)}) copy-start(bf16[32,144,256]{2,1,0:T(8,128)(2,1)S(1)} %get-tuple-element.15.packed.refs_0_) | copy-start | bytes 7077892
  26.9 21.8 %collective-permute-start.5 = (bf16[12,64,256]{2,1,0:T(8,128)(2,1)}, bf16[12,64,256]{2,1,0:T(8,128)(2,1)S(1)}, u32[]{:S(2)}, u32[]{:S(2)}) collective-permute-start(bf16[12,64,256]{2,1,0:T(8,128)(2,1)} %get-tuple-element.21), channel_id=1, source_target_pairs={{0,2},{2,0},{1,3},{3,1},{4,6},{6,4},{5,7},{7,5},{8,10},{10,8},{9,1... | collective-permute-start | bytes 1179656 | tf_op jit(solution)/shard_map/ppermute | solution.py:20
  26.9 31.6 %collective-permute-start.4 = (bf16[12,32,256]{2,1,0:T(8,128)(2,1)}, bf16[12,32,256]{2,1,0:T(8,128)(2,1)}, u32[]{:S(2)}, u32[]{:S(2)}) collective-permute-start(bf16[12,32,256]{2,1,0:T(8,128)(2,1)} %get-tuple-element.20), channel_id=1, source_target_pairs={{0,2},{2,0},{1,3},{3,1},{4,6},{6,4},{5,7},{7,5},{8,10},{10,8},{9,1... | collective-permute-start | bytes 589832 | tf_op jit(solution)/shard_map/ppermute | solution.py:20
  28.4 35.7 %collective-permute-start.3 = (bf16[12,32,256]{2,1,0:T(8,128)(2,1)}, bf16[12,32,256]{2,1,0:T(8,128)(2,1)S(1)}, u32[]{:S(2)}, u32[]{:S(2)}) collective-permute-start(bf16[12,32,256]{2,1,0:T(8,128)(2,1)} %get-tuple-element.18), channel_id=1, source_target_pairs={{0,2},{2,0},{1,3},{3,1},{4,6},{6,4},{5,7},{7,5},{8,10},{10,8},{9,1... | collective-permute-start | bytes 589832 | tf_op jit(solution)/shard_map/ppermute | solution.py:20
  28.6 1.7 %copy-start.2 = (bf16[32,144,256]{2,1,0:T(8,128)(2,1)S(1)}, bf16[32,144,256]{2,1,0:T(8,128)(2,1)}, u32[]{:S(2)}) copy-start(bf16[32,144,256]{2,1,0:T(8,128)(2,1)} %copy-done.1) | copy-start | bytes 7077892

commit v4 on v3

--- a/solution.py
+++ b/solution.py
@@ -34,28 +34,18 @@
 
 def pack_kernel(span, width, targets, groups, place, features, neighbours, *refs):
     packed, last, first, *early = refs[: 3 + targets]
-    held, listed, present, moved, in_sems, out_sems, edge_sems = refs[3 + targets :]
+    present, moved, out_sems, edge_sems = refs[3 + targets :]
     channels = features.shape[0]
     size = span // groups
-    lanes = size * LATS
-    lists = pltpu.make_async_copy(neighbours, listed, in_sems.at[groups])
-    lists.start()
-    loads = []
-    for group in range(groups):
-        part = pl.ds(group * lanes, lanes)
-        loads.append(pltpu.make_async_copy(features.at[:, part], held.at[:, part], in_sems.at[group]))
-        loads[-1].start()
     sort = sorting()
-    lists.wait()
-    slots = LATS + lax.broadcasted_iota(jnp.int32, listed.shape, 1)
-    present[0:TAPS] = jnp.where(listed[...] != slots, 1.0, 0.0).astype(jnp.bfloat16)
-    present[TAPS:] = jnp.zeros((TAP_ROWS - TAPS, listed.shape[1]), jnp.bfloat16)
+    slots = LATS + lax.broadcasted_iota(jnp.int32, neighbours.shape, 1)
+    present[0:TAPS] = jnp.where(neighbours[...] != slots, 1.0, 0.0).astype(jnp.bfloat16)
+    present[TAPS:] = jnp.zeros((TAP_ROWS - TAPS, neighbours.shape[1]), jnp.bfloat16)
     stores = []
     for group in range(groups):
-        loads[group].wait()
         for column in range(group * size, (group + 1) * size):
             at = slice(column * LATS, (column + 1) * LATS)
-            value = jnp.concatenate([held[:, at], present[:, at]], axis=0)
+            value = jnp.concatenate([features[:, at], present[:, at]], axis=0)
             moved[column] = jnp.dot(value, sort, preferred_element_type=jnp.float32).astype(jnp.bfloat16)
         part = pl.ds(group * size, size)
         stores.append(pltpu.make_async_copy(moved.at[part], packed.at[part], out_sems.at[group]))
@@ -79,15 +69,12 @@
     shapes = [(span, rows), (DEG, rows), (DEG, rows)] + [(width, channels)] * targets
     return pl.pallas_call(
         functools.partial(pack_kernel, span, width, targets, groups),
-        in_specs=[SMEM, ANY, ANY],
+        in_specs=[SMEM, VMEM, VMEM],
         out_specs=[ANY] * len(shapes),
         out_shape=[jax.ShapeDtypeStruct(shape + (LATS,), jnp.bfloat16) for shape in shapes],
         scratch_shapes=[
-            pltpu.VMEM(features.shape, jnp.bfloat16),
-            pltpu.VMEM(neighbours.shape, jnp.int32),
             pltpu.VMEM((TAP_ROWS, slot_count), jnp.bfloat16),
             pltpu.VMEM((span, rows, LATS), jnp.bfloat16),
-            pltpu.SemaphoreType.DMA((groups + 1,)),
             pltpu.SemaphoreType.DMA((groups,)),
             pltpu.SemaphoreType.DMA((2 + targets,)),
         ],

time: 70.7 us -> 70.4 us (level)
  no operation moved by 1% of the time
where the time goes in v4:
time: 70.4 us; the launch traced here: 70.2 us
  Pallas kernels  45 us (64%)
  waiting for transfers between devices  12.7 us (18%)
  starting transfers between devices  5.77 us (8%)
  local copies, waits for them, and re-layouts  5.73 us (8%)
  between operations  0.83 us (1%)
    pallas_call x4, Pallas kernels, chunk_step(): pl.pallas_call(functools.partial(chunk_kernel, width, channels, low, last...  40.1 us
    ppermute x6, waiting for transfers between devices, shifted(): return lax.ppermute(value, axis, pairs)  12.7 us
    ppermute x6, starting transfers between devices, shifted(): return lax.ppermute(value, axis, pairs)  5.77 us
    unnamed x12, local copies, waits for them, and re-layouts  5.63 us
    pallas_call x1, Pallas kernels, pack(): pl.pallas_call(functools.partial(pack_kernel, span, width, targets, group...  3.37 us
    pallas_call x1, Pallas kernels, rims_of(): pl.pallas_call(functools.partial(rim_kernel, width, parts), in_specs=[SME...  1.58 us
  transfers between devices with their start and end apart: 6, of which 2 were waited for; matrix products, arithmetic and copies ran while one was open for 0% of the time, Pallas kernels for 50%

profile of v4, /device:TPU:1, one launch (start us, length us, event | category | flops | bytes accessed | tf_op | source)
XLA Modules:
  0.0 70.2 jit_solution(15315801264330000711)
XLA Ops:
  0.0 0.0 copy-start
  0.7 0.1 pad_add_fusion.2.place
  0.8 0.0 copy-start.3
  0.8 1.6 %copy-done.3 = bf16[128,8192]{1,0:T(8,128)(2,1)S(1)} copy-done((bf16[128,8192]{1,0:T(8,128)(2,1)S(1)}, bf16[128,8192]{1,0:T(8,128)(2,1)}, u32[]{:S(2)}) %copy-start.3) | copy-done | bytes 2097176
  2.4 0.0 copy-start.4
  2.4 0.9 %copy-done.4 = s32[8,8192]{1,0:T(8,128)S(1)} copy-done((s32[8,8192]{1,0:T(8,128)S(1)}, s32[8,8192]{1,0:T(8,128)}, u32[]{:S(2)}) %copy-start.4) | copy-done | bytes 262168
  3.4 0.0 copy-start.5
  3.4 3.4 %shard_map.55 = (bf16[32,144,256]{2,1,0:T(8,128)(2,1)S(1)}, bf16[6,144,256]{2,1,0:T(8,128)(2,1)S(1)}, bf16[6,144,256]{2,1,0:T(8,128)(2,1)S(1)}, bf16[16,128,256]{2,1,0:T(8,128)(2,1)}) custom-call(s32[2]{0:T(128)S(1)} %pad_add_fusion.2.place, bf16[128,8192]{1,0:T(8,128)(2,1)S(1)} %copy-done.3, s32[8,8192]{1,0:T(8,128)S(1)} %copy-done.4), custom_call_target="tpu_custom_call" | custom-call | tf_op jit(solution)/shard_map/pallas_call | solution.py:70
  6.7 2.1 %collective-permute-start = (bf16[16,128,256]{2,1,0:T(8,128)(2,1)}, bf16[16,128,256]{2,1,0:T(8,128)(2,1)S(1)}, u32[]{:S(2)}, u32[]{:S(2)}) collective-permute-start(bf16[16,128,256]{2,1,0:T(8,128)(2,1)} %get-tuple-element.14), channel_id=1, source_target_pairs={{0,2},{2,0},{1,3},{3,1},{4,6},{6,4},{5,7},{7,5},{8,10},{10,8},{9,1... | collective-permute-start | bytes 3145736 | tf_op jit(solution)/shard_map/ppermute | solution.py:20
  8.8 2.1 %collective-permute-start.1 = (bf16[6,144,256]{2,1,0:T(8,128)(2,1)S(1)}, bf16[6,144,256]{2,1,0:T(8,128)(2,1)S(1)}, u32[]{:S(2)}, u32[]{:S(2)}) collective-permute-start(bf16[6,144,256]{2,1,0:T(8,128)(2,1)S(1)} %get-tuple-element.16), channel_id=1, source_target_pairs={{0,1},{1,4},{4,5},{5,8},{8,9},{9,12},{12,13},{13,0},{2,3},{3,6},{6... | collective-permute-start | bytes 1327112 | tf_op jit(solution)/shard_map/ppermute | solution.py:20
  11.0 0.0 collective-permute-start.2
  11.0 7.4 %collective-permute-done.1.prev.refs_1_ = bf16[6,144,256]{2,1,0:T(8,128)(2,1)S(1)} collective-permute-done((bf16[6,144,256]{2,1,0:T(8,128)(2,1)S(1)}, bf16[6,144,256]{2,1,0:T(8,128)(2,1)S(1)}, u32[]{:S(2)}, u32[]{:S(2)}) %collective-permute-start.1) | collective-permute-done | bytes 442400 | tf_op jit(solution)/shard_map/ppermute | solution.py:20
  18.4 5.3 %collective-permute-done.2.after.refs_2_ = bf16[6,144,256]{2,1,0:T(8,128)(2,1)S(1)} collective-permute-done((bf16[6,144,256]{2,1,0:T(8,128)(2,1)S(1)}, bf16[6,144,256]{2,1,0:T(8,128)(2,1)S(1)}, u32[]{:S(2)}, u32[]{:S(2)}) %collective-permute-start.2) | collective-permute-done | bytes 442400 | tf_op jit(solution)/shard_map/ppermute | solution.py:20
  23.7 1.6 %shard_map.56 = (bf16[12,64,256]{2,1,0:T(8,128)(2,1)}, bf16[12,32,256]{2,1,0:T(8,128)(2,1)}, bf16[12,32,256]{2,1,0:T(8,128)(2,1)}) custom-call(s32[2]{0:T(128)S(1)} %pad_add_fusion.2.place, bf16[32,144,256]{2,1,0:T(8,128)(2,1)S(1)} %get-tuple-element.15.packed.refs_0_, bf16[6,144,256]{2,1,0:T(8,128)(2,1)S(1)} %collective-permute-done.1.prev.refs_1_, ...), custom_call_target="tpu_custom_call" | custom-call | tf_op jit(solution)/shard_map/pallas_call | solution.py:116
  25.2 0.0 copy-start.1
  25.3 1.4 %copy-done.1 = bf16[32,144,256]{2,1,0:T(8,128)(2,1)} copy-done((bf16[32,144,256]{2,1,0:T(8,128)(2,1)}, bf16[32,144,256]{2,1,0:T(8,128)(2,1)S(1)}, u32[]{:S(2)}) %copy-start.1) | copy-done | bytes 2359320
  26.7 0.0 collective-permute-start.5
  26.7 1.5 %collective-permute-start.4 = (bf16[12,32,256]{2,1,0:T(8,128)(2,1)}, bf16[12,32,256]{2,1,0:T(8,128)(2,1)}, u32[]{:S(2)}, u32[]{:S(2)}) collective-permute-start(bf16[12,32,256]{2,1,0:T(8,128)(2,1)} %get-tuple-element.20), channel_id=1, source_target_pairs={{0,2},{2,0},{1,3},{3,1},{4,6},{6,4},{5,7},{7,5},{8,10},{10,8},{9,1... | collective-permute-start | bytes 589832 | tf_op jit(solution)/shard_map/ppermute | solution.py:20
  28.1 0.0 collective-permute-start.3
  28.2 0.1 pad_add_fusion
  28.3 0.0 copy-done.5
  28.3 0.1 broadcast_in_dim.2.refs_4_
  28.4 0.0 copy-done
  28.4 0.0 copy-start.2
  28.4 1.7 %copy-done.2 = bf16[32,144,256]{2,1,0:T(8,128)(2,1)S(1)} copy-done((bf16[32,144,256]{2,1,0:T(8,128)(2,1)S(1)}, bf16[32,144,256]{2,1,0:T(8,128)(2,1)}, u32[]{:S(2)}) %copy-start.2) | copy-done | bytes 2359320
  30.0 18.4 %shard_map.57 = (f32[16,256,256]{2,1,0:T(8,128)S(1)}, f32[28,32,256]{2,1,0:T(8,128)S(1)}) custom-call(s32[3]{0:T(128)S(1)} %get-tuple-element.24.place, bf16[32,144,256]{2,1,0:T(8,128)(2,1)S(1)} %copy-done.2, bf16[6,144,256]{2,1,0:T(8,128)(2,1)S(1)} %collective-permute-done.1.prev.refs_1_, bf16[6,144,256]{2,1,0:T(8,128)(2,1)S(1)} %collective-permute-done.2.after.refs_2_, ...), custom_call_target="tpu_custom_call" | custom-call | tf_op jit(solution)/shard_map/pallas_call | solution.py:322
  48.4 0.0 collective-permute-done.5.refs_1_
  48.5 0.0 collective-permute-done.refs_0_
  48.5 9.8 %shard_map.58.refs_4_ = f32[16,256,256]{2,1,0:T(8,128)S(1)} custom-call(s32[3]{0:T(128)S(1)} %get-tuple-element.23.place, bf16[16,128,256]{2,1,0:T(8,128)(2,1)S(1)} %collective-permute-done.refs_0_, bf16[12,64,256]{2,1,0:T(8,128)(2,1)S(1)} %collective-permute-done.5.refs_1_, f32[28,32,256]{2,1,0:T(8,128)S(1)} %get-tuple-element.19.refs_2_, ...), custom_call_target="tpu_custom_call" | custom-call | tf_op jit(solution)/shard_map/pallas_call | solution.py:322
  58.2 0.0 collective-permute-done.4.refs_1_
  58.3 5.6 %shard_map.59.refs_4_ = f32[16,256,256]{2,1,0:T(8,128)S(1)} custom-call(s32[3]{0:T(128)S(1)} %get-tuple-element.23.place, bf16[16,128,256]{2,1,0:T(8,128)(2,1)S(1)} %collective-permute-done.refs_0_, bf16[12,32,256]{2,1,0:T(8,128)(2,1)} %collective-permute-done.4.refs_1_, f32[28,32,256]{2,1,0:T(8,128)S(1)} %get-tuple-element.19.refs_2_, ...), custom_call_target="tpu_custom_call" | custom-call | tf_op jit(solution)/shard_map/pallas_call | solution.py:322
  63.8 0.0 collective-permute-done.3.refs_1_
  63.9 6.3 %shard_map.60 = bf16[16,256,256]{2,1,0:T(8,128)(2,1)} custom-call(s32[3]{0:T(128)S(1)} %get-tuple-element.23.place, bf16[16,128,256]{2,1,0:T(8,128)(2,1)S(1)} %collective-permute-done.refs_0_, bf16[12,32,256]{2,1,0:T(8,128)(2,1)S(1)} %collective-permute-done.3.refs_1_, f32[28,32,256]{2,1,0:T(8,128)S(1)} %get-tuple-element.19.refs_2_, ...), custom_call_target="tpu_custom_call" | custom-call | tf_op jit(solution)/shard_map/pallas_call | solution.py:322
Async XLA Ops:
  0.0 28.4 %copy-start = (bf16[7,256,256]{2,1,0:T(8,128)(2,1)S(1)}, bf16[7,256,256]{2,1,0:T(8,128)(2,1)}, u32[]{:S(2)}) copy-start(bf16[7,256,256]{2,1,0:T(8,128)(2,1)} %refs_3_.7) | copy-start | bytes 2752516
  0.8 1.6 %copy-start.3 = (bf16[128,8192]{1,0:T(8,128)(2,1)S(1)}, bf16[128,8192]{1,0:T(8,128)(2,1)}, u32[]{:S(2)}) copy-start(bf16[128,8192]{1,0:T(8,128)(2,1)} %features.1) | copy-start | bytes 6291460
  2.4 0.9 %copy-start.4 = (s32[8,8192]{1,0:T(8,128)S(1)}, s32[8,8192]{1,0:T(8,128)}, u32[]{:S(2)}) copy-start(s32[8,8192]{1,0:T(8,128)} %neighbours.1) | copy-start | bytes 786436
  3.4 24.9 %copy-start.5 = (f32[256]{0:T(256)S(1)}, f32[256]{0:T(256)}, u32[]{:S(2)}) copy-start(f32[256]{0:T(256)} %param.9) | copy-start | bytes 3076
  6.7 41.7 %collective-permute-start = (bf16[16,128,256]{2,1,0:T(8,128)(2,1)}, bf16[16,128,256]{2,1,0:T(8,128)(2,1)S(1)}, u32[]{:S(2)}, u32[]{:S(2)}) collective-permute-start(bf16[16,128,256]{2,1,0:T(8,128)(2,1)} %get-tuple-element.14), channel_id=1, source_target_pairs={{0,2},{2,0},{1,3},{3,1},{4,6},{6,4},{5,7},{7,5},{8,10},{10,8},{9,1... | collective-permute-start | bytes 3145736 | tf_op jit(solution)/shard_map/ppermute | solution.py:20
  8.8 9.5 %collective-permute-start.1 = (bf16[6,144,256]{2,1,0:T(8,128)(2,1)S(1)}, bf16[6,144,256]{2,1,0:T(8,128)(2,1)S(1)}, u32[]{:S(2)}, u32[]{:S(2)}) collective-permute-start(bf16[6,144,256]{2,1,0:T(8,128)(2,1)S(1)} %get-tuple-element.16), channel_id=1, source_target_pairs={{0,1},{1,4},{4,5},{5,8},{8,9},{9,12},{12,13},{13,0},{2,3},{3,6},{6... | collective-permute-start | bytes 1327112 | tf_op jit(solution)/shard_map/ppermute | solution.py:20
  11.0 12.7 %collective-permute-start.2 = (bf16[6,144,256]{2,1,0:T(8,128)(2,1)S(1)}, bf16[6,144,256]{2,1,0:T(8,128)(2,1)S(1)}, u32[]{:S(2)}, u32[]{:S(2)}) collective-permute-start(bf16[6,144,256]{2,1,0:T(8,128)(2,1)S(1)} %get-tuple-element.17), channel_id=1, source_target_pairs={{0,13},{1,0},{4,1},{5,4},{8,5},{9,8},{12,9},{13,12},{2,15},{3,2},{... | collective-permute-start | bytes 1327112 | tf_op jit(solution)/shard_map/ppermute | solution.py:20
  25.2 1.4 %copy-start.1 = (bf16[32,144,256]{2,1,0:T(8,128)(2,1)}, bf16[32,144,256]{2,1,0:T(8,128)(2,1)S(1)}, u32[]{:S(2)}) copy-start(bf16[32,144,256]{2,1,0:T(8,128)(2,1)S(1)} %get-tuple-element.15.packed.refs_0_) | copy-start | bytes 7077892
  26.7 21.8 %collective-permute-start.5 = (bf16[12,64,256]{2,1,0:T(8,128)(2,1)}, bf16[12,64,256]{2,1,0:T(8,128)(2,1)S(1)}, u32[]{:S(2)}, u32[]{:S(2)}) collective-permute-start(bf16[12,64,256]{2,1,0:T(8,128)(2,1)} %get-tuple-element.21), channel_id=1, source_target_pairs={{0,2},{2,0},{1,3},{3,1},{4,6},{6,4},{5,7},{7,5},{8,10},{10,8},{9,1... | collective-permute-start | bytes 1179656 | tf_op jit(solution)/shard_map/ppermute | solution.py:20
  26.7 31.6 %collective-permute-start.4 = (bf16[12,32,256]{2,1,0:T(8,128)(2,1)}, bf16[12,32,256]{2,1,0:T(8,128)(2,1)}, u32[]{:S(2)}, u32[]{:S(2)}) collective-permute-start(bf16[12,32,256]{2,1,0:T(8,128)(2,1)} %get-tuple-element.20), channel_id=1, source_target_pairs={{0,2},{2,0},{1,3},{3,1},{4,6},{6,4},{5,7},{7,5},{8,10},{10,8},{9,1... | collective-permute-start | bytes 589832 | tf_op jit(solution)/shard_map/ppermute | solution.py:20
  28.1 35.7 %collective-permute-start.3 = (bf16[12,32,256]{2,1,0:T(8,128)(2,1)}, bf16[12,32,256]{2,1,0:T(8,128)(2,1)S(1)}, u32[]{:S(2)}, u32[]{:S(2)}) collective-permute-start(bf16[12,32,256]{2,1,0:T(8,128)(2,1)} %get-tuple-element.18), channel_id=1, source_target_pairs={{0,2},{2,0},{1,3},{3,1},{4,6},{6,4},{5,7},{7,5},{8,10},{10,8},{9,1... | collective-permute-start | bytes 589832 | tf_op jit(solution)/shard_map/ppermute | solution.py:20
  28.4 1.7 %copy-start.2 = (bf16[32,144,256]{2,1,0:T(8,128)(2,1)S(1)}, bf16[32,144,256]{2,1,0:T(8,128)(2,1)}, u32[]{:S(2)}) copy-start(bf16[32,144,256]{2,1,0:T(8,128)(2,1)} %copy-done.1) | copy-start | bytes 7077892
